TPU v7x, 32 devices: a whole 2x2x4 slice. The times are simulated.
32 devices in a mesh: dp: 16 (over z, x, core), head: 2 (over y).
Axes of the slice: x: 2, y: 2, z: 4, core: 2. Of those that a mesh axis runs over, the one named last changes fastest.
Arguments:
- tokens: bfloat16 [128, 608, 256], P(('dp', 'head')), may hold values from -6 to 6
- crop_side: int32 [128, 8], P(('dp', 'head')), may hold values from 6 to 14, as said below
- cotangent: bfloat16 [128, 608, 256], P(('dp', 'head')), may hold values from -6 to 6
- ln1_gain: float32 [2, 256], replicated, may hold values from 0.25 to 1.75
- ln1_bias: float32 [2, 256], replicated, may hold values from -1.75 to 1.75
- qkv_weight: bfloat16 [2, 256, 768], replicated, may hold values from -0.5 to 0.5
- lepe_weight: float32 [2, 9, 256], replicated, may hold values from -1.5 to 1.5
- lepe_bias: float32 [2, 256], replicated, may hold values from -3 to 3
- proj_weight: bfloat16 [2, 256, 256], replicated, may hold values from -0.5 to 0.5
- proj_bias: float32 [2, 256], replicated, may hold values from -3 to 3
- ln2_gain: float32 [2, 256], replicated, may hold values from 0.25 to 1.75
- ln2_bias: float32 [2, 256], replicated, may hold values from -1.75 to 1.75
- fc1_weight: bfloat16 [2, 256, 1024], replicated, may hold values from -0.375 to 0.375
- fc1_bias: float32 [2, 1024], replicated, may hold values from -3 to 3
- fc2_weight: bfloat16 [2, 1024, 256], replicated, may hold values from -0.25 to 0.25
- fc2_bias: float32 [2, 256], replicated, may hold values from -3 to 3
Outputs:
- out: bfloat16 [128, 608, 256], P(('dp', 'head'))
- input_grad: float32 [128, 608, 256], P(('dp', 'head'))
- ln1_gain_grad: float32 [2, 256], replicated
- ln1_bias_grad: float32 [2, 256], replicated
- qkv_weight_grad: float32 [2, 256, 768], replicated
- lepe_weight_grad: float32 [2, 9, 256], replicated
- lepe_bias_grad: float32 [2, 256], replicated
- proj_weight_grad: float32 [2, 256, 256], replicated
- proj_bias_grad: float32 [2, 256], replicated
- ln2_gain_grad: float32 [2, 256], replicated
- ln2_bias_grad: float32 [2, 256], replicated
- fc1_weight_grad: float32 [2, 256, 1024], replicated
- fc1_bias_grad: float32 [2, 1024], replicated
- fc2_weight_grad: float32 [2, 1024, 256], replicated
- fc2_bias_grad: float32 [2, 256], replicated
Inputs may be any that keep to these rules, and one draw needn't show every extreme that they name: `crop_side`: each image has 2 crops of side 14 and 6 crops of side 6, in an order drawn for each image.
All inputs are finite; a program needn't handle non-finite values.
Results may differ from a plain program's by a relative error of at most 0.017.
Values may be sent and summed in bfloat16 or wider, within the bound.
A program may use at most 192 MiB of HBM per device.

v0:
```python
from functools import partial
import math

import jax
import jax.numpy as jnp
from jax import lax
from jax.sharding import PartitionSpec as P

HEAD_DIM = 32
SW = 7
TOK_IMG = 608


EPSILON = 1e-05


def shortened(value):

    def short(part):
        return part.astype(jnp.bfloat16) if part.dtype == jnp.float32 else part

    return jax.tree.map(short, value)


def normalize(values, gain_vec, shift_vec):
    center = values - jnp.mean(values, axis=-1, keepdims=True)
    spread = jnp.mean(center * center, axis=-1, keepdims=True)
    return center * lax.rsqrt(spread + EPSILON) * gain_vec + shift_vec


def gelu_exact(values):
    return jax.nn.gelu(values, approximate=False)


def layout(sides):
    crop_area = sides * sides
    crop_ends = jnp.cumsum(crop_area)
    crop_starts = crop_ends - crop_area
    positions = jnp.arange(TOK_IMG, dtype=jnp.int32)
    crop_of = jnp.sum((positions[:, None] >= crop_ends[None, :]).astype(jnp.int32), axis=1)
    chosen = (crop_of[:, None] == jnp.arange(sides.shape[0], dtype=jnp.int32)[None, :]).astype(
        jnp.int32
    )
    start_of = jnp.sum(chosen * crop_starts[None, :], axis=1)
    side_of = jnp.sum(chosen * sides[None, :], axis=1)
    offset = positions - start_of
    return (positions, crop_of, offset // side_of, offset % side_of, side_of, start_of)


def windows(sides, vertical):
    positions, crop_of, row_of, column_of, side_of, start_of = layout(sides)
    stripe_of = jnp.where(vertical, column_of // SW, row_of // SW)
    window = crop_of * TOK_IMG + stripe_of
    places = []
    usable = []
    for step_row in (-1, 0, 1):
        for step_col in (-1, 0, 1):
            row_to = row_of + step_row
            column_to = column_of + step_col
            inside = (row_to >= 0) & (row_to < side_of) & (column_to >= 0) & (column_to < side_of)
            stripe_to = jnp.where(vertical, column_to // SW, row_to // SW)
            usable_now = inside & (stripe_to == stripe_of)
            places.append(jnp.where(usable_now, start_of + row_to * side_of + column_to, positions))
            usable.append(usable_now)
    return (window, jnp.stack(places), jnp.stack(usable).astype(jnp.float32))


def masked_scores(queries, keys_in, window):
    raw = jnp.einsum(
        "thd,uhd->htu", queries, keys_in, preferred_element_type=jnp.float32
    ) * HEAD_DIM ** (-0.5)
    allowed = window[:, None] == window[None, :]
    return jnp.where(allowed[None], raw, -1e30)


def group_forward(group_part, sides, vertical, lepe_w, lepe_b):
    group_width = group_part.shape[2]
    group_heads = group_width // HEAD_DIM
    window, places, usable = windows(sides, vertical)
    queries = group_part[:, 0].reshape(TOK_IMG, group_heads, HEAD_DIM)
    keys_in = group_part[:, 1].reshape(TOK_IMG, group_heads, HEAD_DIM)
    values_in = group_part[:, 2]
    scores = masked_scores(queries, keys_in, window)
    row_max = jnp.max(scores, axis=-1, keepdims=True)
    row_total = jnp.sum(jnp.exp(scores - row_max), axis=-1, keepdims=True)
    log_sums = row_max + jnp.log(row_total)
    probabilities = jnp.exp(scores - log_sums).astype(jnp.bfloat16)
    mixed = jnp.einsum(
        "htu,uhd->thd",
        probabilities,
        values_in.reshape(TOK_IMG, group_heads, HEAD_DIM),
        preferred_element_type=jnp.float32,
    )
    neighbours_v = jnp.take(values_in, places, axis=0).astype(jnp.float32)
    lepe_term = jnp.sum(lepe_w[:, None, :] * neighbours_v * usable[:, :, None], axis=0)
    combined = mixed.reshape(TOK_IMG, group_width) + lepe_term + lepe_b
    return (combined.astype(jnp.bfloat16), log_sums[:, :, 0])


def group_backward(group_part, sides, vertical, lepe_w, log_sums, grad_out):
    group_width = group_part.shape[2]
    group_heads = group_width // HEAD_DIM
    window, places, usable = windows(sides, vertical)
    queries = group_part[:, 0].reshape(TOK_IMG, group_heads, HEAD_DIM)
    keys_in = group_part[:, 1].reshape(TOK_IMG, group_heads, HEAD_DIM)
    values_in = group_part[:, 2]
    values_heads = values_in.reshape(TOK_IMG, group_heads, HEAD_DIM)
    scores = masked_scores(queries, keys_in, window)
    probs_full = jnp.exp(scores - log_sums[:, :, None])
    probabilities = probs_full.astype(jnp.bfloat16)
    grad_heads = grad_out.reshape(TOK_IMG, group_heads, HEAD_DIM)
    grad_values = jnp.einsum(
        "htu,thd->uhd", probabilities, grad_heads, preferred_element_type=jnp.float32
    ).reshape(TOK_IMG, group_width)
    grad_probs = jnp.einsum(
        "thd,uhd->htu", grad_heads, values_heads, preferred_element_type=jnp.float32
    )
    row_inner = jnp.sum(probs_full * grad_probs, axis=-1, keepdims=True)
    grad_scores = (probs_full * (grad_probs - row_inner)).astype(jnp.bfloat16)
    score_scale = HEAD_DIM ** (-0.5)
    grad_queries = (
        jnp.einsum("htu,uhd->thd", grad_scores, keys_in, preferred_element_type=jnp.float32)
        * score_scale
    )
    grad_keys = (
        jnp.einsum("htu,thd->uhd", grad_scores, queries, preferred_element_type=jnp.float32)
        * score_scale
    )
    grad_float = grad_out.astype(jnp.float32)
    back_near = jnp.take(grad_float, places[::-1], axis=0)
    grad_values = grad_values + jnp.sum(
        lepe_w[:, None, :] * back_near * usable[::-1][:, :, None], axis=0
    )
    neighbours_v = jnp.take(values_in, places, axis=0).astype(jnp.float32)
    lepe_w_grad = jnp.sum(neighbours_v * usable[:, :, None] * grad_float[None], axis=1)
    lepe_b_grad = jnp.sum(grad_float, axis=0)
    packed_grad = jnp.stack(
        [
            grad_queries.reshape(TOK_IMG, group_width),
            grad_keys.reshape(TOK_IMG, group_width),
            grad_values,
        ],
        axis=1,
    )
    return (packed_grad.astype(jnp.bfloat16), lepe_w_grad, lepe_b_grad)


def own_forward(item_pair, vertical, lepe_w, lepe_b):
    return group_forward(item_pair[0], item_pair[1], vertical, lepe_w, lepe_b)


def own_backward(item_four, vertical, lepe_w):
    return group_backward(item_four[0], item_four[1], vertical, lepe_w, item_four[2], item_four[3])


def stack_member(layer_grads, position):
    return jnp.stack([entry[position] for entry in layer_grads])


def local(
    tokens,
    crop_side,
    cotangent,
    ln1_gain,
    ln1_bias,
    qkv_weight,
    lepe_weight,
    lepe_bias,
    proj_weight,
    proj_bias,
    ln2_gain,
    ln2_bias,
    fc1_weight,
    fc1_bias,
    fc2_weight,
    fc2_bias,
):
    layer_count = qkv_weight.shape[0]
    model_width = tokens.shape[2]
    group_width = model_width // lax.axis_size("head")
    group_index = lax.axis_index("head")
    vertical = group_index == 1
    images_here = tokens.shape[0]
    sides_here = lax.all_gather(crop_side, "head", axis=0, tiled=True)
    current = tokens.astype(jnp.float32)
    saved = []
    for layer_idx in range(layer_count):
        w_qkv = qkv_weight[layer_idx]
        w_lepe = lepe_weight[layer_idx]
        b_lepe = lepe_bias[layer_idx]
        normed = normalize(current, ln1_gain[layer_idx], ln1_bias[layer_idx]).astype(jnp.bfloat16)
        packed = jnp.einsum(
            "itd,de->ite", normed, w_qkv, preferred_element_type=jnp.float32
        ).astype(jnp.bfloat16)
        packed = packed.reshape(packed.shape[0], packed.shape[1], 3, model_width)
        heads_in = lax.all_to_all(packed, "head", split_axis=3, concat_axis=0, tiled=True)
        lepe_w_part = lax.dynamic_slice_in_dim(w_lepe, group_index * group_width, group_width, 1)
        lepe_b_part = lax.dynamic_slice_in_dim(b_lepe, group_index * group_width, group_width, 0)
        heads_out, log_sums = lax.map(
            partial(own_forward, vertical=vertical, lepe_w=lepe_w_part, lepe_b=lepe_b_part),
            (heads_in, sides_here),
        )
        merged = jax.tree.map(
            lambda part, own: part.astype(own.dtype),
            lax.all_to_all(shortened(heads_out), "head", split_axis=0, concat_axis=2, tiled=True),
            heads_out,
        )
        middle = (
            current
            + jnp.einsum(
                "itd,de->ite", merged, proj_weight[layer_idx], preferred_element_type=jnp.float32
            )
            + proj_bias[layer_idx]
        )
        normed_two = normalize(middle, ln2_gain[layer_idx], ln2_bias[layer_idx]).astype(
            jnp.bfloat16
        )
        hidden = (
            jnp.einsum(
                "itd,df->itf", normed_two, fc1_weight[layer_idx], preferred_element_type=jnp.float32
            )
            + fc1_bias[layer_idx]
        )
        active = gelu_exact(hidden).astype(jnp.bfloat16)
        saved.append((current, heads_in, log_sums, merged, middle, hidden))
        current = (
            middle
            + jnp.einsum(
                "itf,fd->itd", active, fc2_weight[layer_idx], preferred_element_type=jnp.float32
            )
            + fc2_bias[layer_idx]
        )
    result = current.astype(jnp.bfloat16)
    upstream = cotangent.astype(jnp.float32)
    layer_grads = [None] * layer_count
    for layer_idx in reversed(range(layer_count)):
        w_qkv = qkv_weight[layer_idx]
        w_lepe = lepe_weight[layer_idx]
        w_proj = proj_weight[layer_idx]
        w_up = fc1_weight[layer_idx]
        w_down = fc2_weight[layer_idx]
        state_in, heads_in, log_sums, merged, middle, hidden = saved[layer_idx]
        down_in = upstream.astype(jnp.bfloat16)
        active = gelu_exact(hidden).astype(jnp.bfloat16)
        g_down = jnp.einsum("itf,itd->fd", active, down_in, preferred_element_type=jnp.float32)
        g_down_b = jnp.sum(down_in.astype(jnp.float32), axis=(0, 1))
        grad_active = jnp.einsum("itd,fd->itf", down_in, w_down, preferred_element_type=jnp.float32)
        unused, gelu_pull = jax.vjp(gelu_exact, hidden)
        grad_hidden = gelu_pull(grad_active)[0].astype(jnp.bfloat16)
        normed_two, norm_pull_two = jax.vjp(
            normalize, middle, ln2_gain[layer_idx], ln2_bias[layer_idx]
        )
        g_up = jnp.einsum(
            "itd,itf->df",
            normed_two.astype(jnp.bfloat16),
            grad_hidden,
            preferred_element_type=jnp.float32,
        )
        g_up_b = jnp.sum(grad_hidden.astype(jnp.float32), axis=(0, 1))
        grad_normed_two = jnp.einsum(
            "itf,df->itd", grad_hidden, w_up, preferred_element_type=jnp.float32
        )
        grad_middle, g_gain_b, g_shift_b = norm_pull_two(grad_normed_two)
        grad_middle = grad_middle + upstream
        proj_in = grad_middle.astype(jnp.bfloat16)
        g_proj = jnp.einsum("itd,ite->de", merged, proj_in, preferred_element_type=jnp.float32)
        g_proj_b = jnp.sum(proj_in.astype(jnp.float32), axis=(0, 1))
        grad_merged = jnp.einsum(
            "ite,de->itd", proj_in, w_proj, preferred_element_type=jnp.float32
        ).astype(jnp.bfloat16)
        grad_heads = lax.all_to_all(grad_merged, "head", split_axis=2, concat_axis=0, tiled=True)
        lepe_w_part = lax.dynamic_slice_in_dim(w_lepe, group_index * group_width, group_width, 1)
        grad_packed, weight_terms, bias_terms = lax.map(
            partial(own_backward, vertical=vertical, lepe_w=lepe_w_part),
            (heads_in, sides_here, log_sums, grad_heads),
        )
        g_lepe = lax.dynamic_update_slice_in_dim(
            jnp.zeros((9, model_width), jnp.float32),
            jnp.sum(weight_terms, axis=0),
            group_index * group_width,
            1,
        )
        g_lepe_b = lax.dynamic_update_slice_in_dim(
            jnp.zeros((model_width,), jnp.float32),
            jnp.sum(bias_terms, axis=0),
            group_index * group_width,
            0,
        )
        grad_home = jax.tree.map(
            lambda part, own: part.astype(own.dtype),
            lax.all_to_all(shortened(grad_packed), "head", split_axis=0, concat_axis=3, tiled=True),
            grad_packed,
        )
        grad_home = grad_home.reshape(grad_home.shape[0], grad_home.shape[1], 3 * model_width)
        normed_one, norm_pull_one = jax.vjp(
            normalize, state_in, ln1_gain[layer_idx], ln1_bias[layer_idx]
        )
        g_qkv = jnp.einsum(
            "itd,ite->de",
            normed_one.astype(jnp.bfloat16),
            grad_home,
            preferred_element_type=jnp.float32,
        )
        grad_normed_one = jnp.einsum(
            "ite,de->itd", grad_home, w_qkv, preferred_element_type=jnp.float32
        )
        grad_state, g_gain_a, g_shift_a = norm_pull_one(grad_normed_one)
        upstream = grad_state + grad_middle
        layer_grads[layer_idx] = (
            g_gain_a,
            g_shift_a,
            g_qkv,
            g_lepe,
            g_lepe_b,
            g_proj,
            g_proj_b,
            g_gain_b,
            g_shift_b,
            g_up,
            g_up_b,
            g_down,
            g_down_b,
        )
    (
        all_gain_a,
        all_shift_a,
        all_qkv,
        all_lepe_w,
        all_lepe_b,
        all_proj,
        all_proj_b,
        all_gain_b,
        all_shift_b,
        all_up,
        all_up_b,
        all_down,
        all_down_b,
    ) = [stack_member(layer_grads, position) for position in range(13)]
    (
        all_gain_a,
        all_shift_a,
        all_qkv,
        all_lepe_w,
        all_lepe_b,
        all_proj,
        all_proj_b,
        all_gain_b,
        all_shift_b,
        all_up,
        all_up_b,
        all_down,
        all_down_b,
    ) = lax.psum(
        (
            all_gain_a,
            all_shift_a,
            all_qkv,
            all_lepe_w,
            all_lepe_b,
            all_proj,
            all_proj_b,
            all_gain_b,
            all_shift_b,
            all_up,
            all_up_b,
            all_down,
            all_down_b,
        ),
        ("dp", "head"),
    )
    factor = 1.0 / math.sqrt(lax.axis_size("dp") * lax.axis_size("head") * images_here * TOK_IMG)
    return (
        result,
        upstream,
        all_gain_a * factor,
        all_shift_a * factor,
        all_qkv * factor,
        all_lepe_w * factor,
        all_lepe_b * factor,
        all_proj * factor,
        all_proj_b * factor,
        all_gain_b * factor,
        all_shift_b * factor,
        all_up * factor,
        all_up_b * factor,
        all_down * factor,
        all_down_b * factor,
    )


def solution(mesh):
    return jax.shard_map(
        local,
        mesh=mesh,
        in_specs=(
            P(("dp", "head"), None, None),
            P(("dp", "head"), None),
            P(("dp", "head"), None, None),
            P(),
            P(),
            P(),
            P(),
            P(),
            P(),
            P(),
            P(),
            P(),
            P(),
            P(),
            P(),
            P(),
        ),
        out_specs=(
            P(("dp", "head"), None, None),
            P(("dp", "head"), None, None),
            P(),
            P(),
            P(),
            P(),
            P(),
            P(),
            P(),
            P(),
            P(),
            P(),
            P(),
            P(),
            P(),
        ),
        check_vma=False,
    )
```

profile of v0, /device:TPU:0, one launch (start us, length us, event | category | flops | bytes accessed | tf_op | source)
XLA Modules:
  0.0 2016.0 jit_solution(8873738648374183480)
XLA Ops:
  36.9 46.0 %all-gather = s32[2,4,8]{2,1,0:T(4,128)S(1)} all-gather(s32[1,4,8]{2,1,0:T(4,128)S(1)} %bitcast.657), channel_id=1, replica_groups=mesh['dp'=16,'head'=2] {'head'}, dimensions={0}, use_global_device_ids=true | all-gather | bytes 384 | tf_op jit(solution)/shard_map/all_gather | solution.py:184
  96.2 208.6 %while.64 = (s32[]{:T(128)}, bf16[8,608,128]{2,1,0:T(8,128)(2,1)}, f32[8,4,608]{2,1,0:T(4,128)S(1)}, bf16[8,608,3,128]{3,1,2,0:T(8,128)(2,1)}, s32[8,8]{1,0:T(8,...) while((s32[]{:T(128)}, bf16[8,608,128]{2,1,0:T(8,128)(2,1)}, ...), condition=%wide.region_10.12_spmd, body=%wide.region_2.11_spmd.sunk | while | flops 209785072 | bytes 53041844 | solution.py:199
  98.7 10.9 gather_fusion
  124.7 10.9 gather_fusion
  150.8 10.9 gather_fusion
  176.9 10.9 gather_fusion
  203.0 10.9 gather_fusion
  229.0 10.9 gather_fusion
  255.1 10.9 gather_fusion
  281.2 10.9 gather_fusion
  309.7 14.9 all-to-all-done.1
  336.9 24.0 %multiply_convert_fusion.3 = (bf16[4,608,1024]{2,1,0:T(8,128)(2,1)S(1)}, f32[4,608,1024]{2,1,0:T(8,128)}) fusion(f32[4,608,1024]{2,1,0:T(8,128)S(1)} %get-tuple-element.999, f32[1024]{0:T(1024)S(1)} %bitcast.630, u8[608,1024]{1,0:T(8,128)(4,1)S(1)} %get-tuple-element.624, u8[608,1024]{1,0:T(8,128)(4,1)S(1)} %get-tuple-element.623), kind=kLoop, calls=%fused_computation.474 | loop fusion | flops 176816128 | bytes 26152960 | tf_op jit(solution)/shard_map/convert_element_type | solution.py:224
  387.0 43.6 %all-to-all-done.2 = bf16[4,608,3,256]{1,0,2,3:T(4,128)(2,1)} async-done(((bf16[4,608,3,256]{1,0,2,3:T(4,128)(2,1)}), bf16[4,608,3,256]{1,0,2,3:T(4,128)(2,1)}, u32[]{:S(2)}, u32[]{:S(2)}) %all-to-all-start.2) | async-done | bytes 3735584 | tf_op jit(solution)/shard_map/all_to_all | solution.py:196
  442.8 208.2 %while.65 = (s32[]{:T(128)}, bf16[8,608,128]{2,1,0:T(8,128)(2,1)}, f32[8,4,608]{2,1,0:T(4,128)S(1)}, bf16[8,608,3,128]{3,1,2,0:T(8,128)(2,1)}, s32[8,8]{1,0:T(8,...) while((s32[]{:T(128)}, bf16[8,608,128]{2,1,0:T(8,128)(2,1)}, ...), condition=%wide.region_23.25_spmd, body=%wide.region_15.24_spmd.sunk | while | flops 209785072 | bytes 53041844 | solution.py:199
  445.2 10.9 gather_fusion.1
  471.3 10.9 gather_fusion.1
  497.3 10.9 gather_fusion.1
  523.3 10.9 gather_fusion.1
  549.3 10.9 gather_fusion.1
  575.4 10.9 gather_fusion.1
  601.4 10.9 gather_fusion.1
  627.4 10.9 gather_fusion.1
  651.6 17.8 all_to_all.138
  683.4 24.2 %multiply_convert_fusion.2 = (bf16[4,608,1024]{2,1,0:T(8,128)(2,1)}, f32[4,608,1024]{2,1,0:T(8,128)}) fusion(f32[4,608,1024]{2,1,0:T(8,128)S(1)} %get-tuple-element.1004, f32[1024]{0:T(1024)S(1)} %bitcast.633, u8[608,1024]{1,0:T(8,128)(4,1)S(1)} %get-tuple-element.622, u8[608,1024]{1,0:T(8,128)(4,1)S(1)} %get-tuple-element.621), kind=kLoop, calls=%fused_computation.461 | loop fusion | flops 176816128 | bytes 26152960 | tf_op jit(solution)/shard_map/convert_element_type | solution.py:224
  749.3 447.1 %while.66 = (s32[]{:T(128)}, bf16[8,608,3,128]{3,1,2,0:T(8,128)(2,1)}, f32[8,9,128]{2,1,0:T(8,128)S(1)}, f32[8,128]{1,0:T(8,128)}, bf16[8,608,3,128]{3,1,2,0:T(8...) while((s32[]{:T(128)}, ...), condition=%wide.region_37.40_spmd, body=%wide.region_28.39_spmd.sunk | while | flops 504325216 | bytes 95596992 | solution.py:273
  752.1 10.9 gather_fusion.3
  787.0 8.9 gather_fusion.2
  808.0 10.9 gather_fusion.3
  842.9 8.9 gather_fusion.2
  863.9 10.9 gather_fusion.3
  898.7 8.9 gather_fusion.2
  919.7 10.9 gather_fusion.3
  954.6 8.9 gather_fusion.2
  975.5 10.9 gather_fusion.3
  1010.4 8.9 gather_fusion.2
  1031.4 10.9 gather_fusion.3
  1066.3 8.9 gather_fusion.2
  1087.3 10.9 gather_fusion.3
  1122.1 8.9 gather_fusion.2
  1143.1 10.9 gather_fusion.3
  1178.0 8.9 gather_fusion.2
  1215.1 26.5 %all-to-all-done.5 = bf16[8,608,3,128]{3,1,2,0:T(8,128)(2,1)} async-done(((bf16[8,608,3,128]{3,1,2,0:T(8,128)(2,1)}), bf16[8,608,3,128]{3,1,2,0:T(8,128)(2,1)}, u32[]{:S(2)}, u32[]{:S(2)}) %all-to-all-start.5) | async-done | bytes 3735584 | tf_op jit(solution)/shard_map/all_to_all | solution.py:291
  1249.5 9.6 reshape.4746
  1267.6 10.3 convert_reduce_fusion.7
  1312.5 464.2 %while.67 = (s32[]{:T(128)}, bf16[8,608,3,128]{3,1,2,0:T(8,128)(2,1)}, f32[8,9,128]{2,1,0:T(8,128)S(1)}, f32[8,128]{1,0:T(8,128)}, bf16[8,608,3,128]{3,1,2,0:T(8...) while((s32[]{:T(128)}, ...), condition=%wide.region_51.54_spmd, body=%wide.region_42.53_spmd.sunk | while | flops 504325216 | bytes 94972232 | solution.py:273
  1316.5 10.9 gather_fusion.5
  1352.4 8.9 gather_fusion.4
  1374.5 10.9 gather_fusion.5
  1410.4 8.9 gather_fusion.4
  1432.5 10.9 gather_fusion.5
  1468.4 8.9 gather_fusion.4
  1490.5 10.9 gather_fusion.5
  1526.5 8.9 gather_fusion.4
  1548.5 10.9 gather_fusion.5
  1584.5 8.9 gather_fusion.4
  1606.5 10.9 gather_fusion.5
  1642.5 8.9 gather_fusion.4
  1664.5 10.9 gather_fusion.5
  1722.5 10.9 gather_fusion.5
  1758.4 8.9 gather_fusion.4
  1793.3 26.4 %all-to-all-done.7 = bf16[8,608,3,128]{3,1,2,0:T(8,128)(2,1)} async-done(((bf16[8,608,3,128]{3,1,2,0:T(8,128)(2,1)}), bf16[8,608,3,128]{3,1,2,0:T(8,128)(2,1)}, u32[]{:S(2)}, u32[]{:S(2)}) %all-to-all-start.7) | async-done | bytes 3735584 | tf_op jit(solution)/shard_map/all_to_all | solution.py:291
  1827.5 9.6 reshape.4747
  1848.2 39.3 %all-reduce = (f32[2,256]{1,0:T(2,128)S(1)}, f32[2,256]{1,0:T(2,128)S(1)}, f32[2,9,256]{2,0,1:T(2,128)S(1)}, f32[2,256]{1,0:T(2,128)S(1)}, f32[2,256]{1,0:T(2,12...) all-reduce(f32[2,256]{1,0:T(2,128)S(1)} %pad_maximum_fusion.6, ...), channel_id=1, replica_groups=mesh['dp'=16,'head'=2] {'dp','head'}, use_global_device_ids=true, to_apply=%region_56.59 | all-reduce | flops 10240 | bytes 81920 | tf_op jit(solution)/shard_map/psum | solution.py:353
  1898.7 103.0 %all-reduce.4.cloned.1.call-done = (f32[2,256,768]{2,1,0:T(8,128)}, f32[2,256,256]{2,1,0:T(8,128)}, f32[2,256,1024]{2,1,0:T(8,128)}, f32[2,1024,256]{2,1,0:T(8,128)}) async-done(((f32[2,256,768]{2,1,0:T(8,128)}, f32[2,256,256]{2,1,0:T(8,128)}, f32[2,256,1024]{2,1,0:T(8,128)}, f32[2,1024,256]{2,1,0:T(8,128)}), (f32[2,256,768]{2,1,0:T(8,128)}, f32[2,256,256]{2,1,0:T(8,128)}, f32[2,256,1024]{2,1,0:T(8,128)}, ...) | async-done | bytes 6291472 | tf_op jit(solution)/shard_map/psum | solution.py:353
  (2243 shorter events, 1113.2 us)
Async XLA Ops:
  12.4 352.1 %copy-start.111 = (f32[1,256]{1,0:T(1,128)}, f32[1,256]{1,0:T(1,128)S(1)}, u32[]{:S(2)}) copy-start(f32[1,256]{1,0:T(1,128)S(1)} %get-tuple-element.993) | copy-start | bytes 3076
  13.1 351.4 %copy-start.139 = (f32[1,256]{1,0:T(1,128)}, f32[1,256]{1,0:T(1,128)S(1)}, u32[]{:S(2)}) copy-start(f32[1,256]{1,0:T(1,128)S(1)} %get-tuple-element.995) | copy-start | bytes 3076
  31.1 51.8 %copy-start.142 = (f32[2,256]{1,0:T(2,128)S(1)}, f32[2,256]{1,0:T(2,128)}, u32[]{:S(2)}) copy-start(f32[2,256]{1,0:T(2,128)} %param.35) | copy-start | bytes 6148
  31.1 51.8 %copy-start.143 = (f32[2,256]{1,0:T(2,128)S(1)}, f32[2,256]{1,0:T(2,128)}, u32[]{:S(2)}) copy-start(f32[2,256]{1,0:T(2,128)} %param.37) | copy-start | bytes 6148
  31.1 52.4 %copy-start.144 = (f32[2,256]{1,0:T(2,128)S(1)}, f32[2,256]{1,0:T(2,128)}, u32[]{:S(2)}) copy-start(f32[2,256]{1,0:T(2,128)} %param.38) | copy-start | bytes 6148
  31.1 53.0 %all-to-all-start = ((bf16[4,608,3,256]{1,0,2,3:T(4,128)(2,1)}), bf16[4,608,3,256]{1,0,2,3:T(4,128)(2,1)}, u32[]{:S(2)}, u32[]{:S(2)}) async-start(bf16[4,608,3,256]{1,0,2,3:T(4,128)(2,1)} %copy.262), calls=%async_computation | async-start | bytes 7864320 | tf_op jit(solution)/shard_map/all_to_all | solution.py:196
  84.1 247.8 %copy-start.117 = (f32[1,256]{1,0:T(1,128)}, f32[1,256]{1,0:T(1,128)S(1)}, u32[]{:S(2)}) copy-start(f32[1,256]{1,0:T(1,128)S(1)} %get-tuple-element.986) | copy-start | bytes 3076
  96.2 212.9 %copy-start.145 = (f32[2,256]{1,0:T(2,128)S(1)}, f32[2,256]{1,0:T(2,128)}, u32[]{:S(2)}) copy-start(f32[2,256]{1,0:T(2,128)} %param.39) | copy-start | bytes 6148
  96.2 212.9 %copy-start.146 = (f32[2,256]{1,0:T(2,128)S(1)}, f32[2,256]{1,0:T(2,128)}, u32[]{:S(2)}) copy-start(f32[2,256]{1,0:T(2,128)} %param.43) | copy-start | bytes 6148
  96.2 213.5 %copy-start.133 = (f32[2,1024]{1,0:T(2,128)S(1)}, f32[2,1024]{1,0:T(2,128)}, u32[]{:S(2)}) copy-start(f32[2,1024]{1,0:T(2,128)} %param.41) | copy-start | bytes 24580
  305.4 19.2 all-to-all-start.1
  309.1 21.3 %copy-start.21 = (bf16[4,608,256]{2,1,0:T(8,128)(2,1)S(1)}, bf16[4,608,256]{2,1,0:T(8,128)(2,1)}, u32[]{:S(2)}) copy-start(bf16[4,608,256]{2,1,0:T(8,128)(2,1)} %param.28) | copy-start | bytes 3735556
  309.1 21.3 %copy-start.55 = (bf16[2,256,256]{2,1,0:T(8,128)(2,1)S(1)}, bf16[2,256,256]{2,1,0:T(8,128)(2,1)}, u32[]{:S(2)}) copy-start(bf16[2,256,256]{2,1,0:T(8,128)(2,1)} %param.36) | copy-start | bytes 786436
  309.1 22.8 %copy-start.126 = (f32[1,256]{1,0:T(1,128)}, f32[1,256]{1,0:T(1,128)S(1)}, u32[]{:S(2)}) copy-start(f32[1,256]{1,0:T(1,128)S(1)} %get-tuple-element.988) | copy-start | bytes 3076
  309.1 369.5 %copy-start.127 = (f32[1,256]{1,0:T(1,128)}, f32[1,256]{1,0:T(1,128)S(1)}, u32[]{:S(2)}) copy-start(f32[1,256]{1,0:T(1,128)S(1)} %get-tuple-element.987) | copy-start | bytes 3076
  309.7 27.1 %copy-start.122 = (f32[1,1024]{1,0:T(1,128)}, f32[1,1024]{1,0:T(1,128)S(1)}, u32[]{:S(2)}) copy-start(f32[1,1024]{1,0:T(1,128)S(1)} %get-tuple-element.982) | copy-start | bytes 12292
  331.1 29.8 %copy-start.10 = (f32[4,608,256]{2,1,0:T(8,128)}, f32[4,608,256]{2,1,0:T(8,128)S(1)}, u32[]{:S(2)}) copy-start(f32[4,608,256]{2,1,0:T(8,128)S(1)} %get-tuple-element.998) | copy-start | bytes 7471108
  336.8 24.0 %copy-start.42 = (f32[4,608,1024]{2,1,0:T(8,128)}, f32[4,608,1024]{2,1,0:T(8,128)S(1)}, u32[]{:S(2)}) copy-start(f32[4,608,1024]{2,1,0:T(8,128)S(1)} %get-tuple-element.999) | copy-start | bytes 29884420
  336.9 24.0 %copy-start.154 = (bf16[2,1024,256]{2,1,0:T(8,128)(2,1)S(1)}, bf16[2,1024,256]{2,1,0:T(8,128)(2,1)}, u32[]{:S(2)}) copy-start(bf16[2,1024,256]{2,1,0:T(8,128)(2,1)} %param.42) | copy-start | bytes 3145732
  381.5 49.1 %all-to-all-start.2 = ((bf16[4,608,3,256]{1,0,2,3:T(4,128)(2,1)}), bf16[4,608,3,256]{1,0,2,3:T(4,128)(2,1)}, u32[]{:S(2)}, u32[]{:S(2)}) async-start(bf16[4,608,3,256]{1,0,2,3:T(4,128)(2,1)} %copy.268), calls=%async_computation.2 | async-start | bytes 7864320 | tf_op jit(solution)/shard_map/all_to_all | solution.py:196
  677.8 41.1 %copy-start.13 = (f32[4,608,256]{2,1,0:T(8,128)}, f32[4,608,256]{2,1,0:T(8,128)S(1)}, u32[]{:S(2)}) copy-start(f32[4,608,256]{2,1,0:T(8,128)S(1)} %get-tuple-element.1003) | copy-start | bytes 7471108
  677.9 41.1 %copy-start.68 = (f32[4,608]{1,0:T(4,128)}, f32[4,608]{1,0:T(4,128)S(1)}, u32[]{:S(2)}) copy-start(f32[4,608]{1,0:T(4,128)S(1)} %broadcast_multiply_fusion.5) | copy-start | bytes 29188
  678.6 40.3 %copy-start.75 = (f32[4,608]{1,0:T(4,128)}, f32[4,608]{1,0:T(4,128)S(1)}, u32[]{:S(2)}) copy-start(f32[4,608]{1,0:T(4,128)S(1)} %fusion.159) | copy-start | bytes 29188
  683.3 24.2 %copy-start.44 = (bf16[4,608,256]{2,1,0:T(8,128)(2,1)S(1)}, bf16[4,608,256]{2,1,0:T(8,128)(2,1)}, u32[]{:S(2)}) copy-start(bf16[4,608,256]{2,1,0:T(8,128)(2,1)} %param.30) | copy-start | bytes 3735556
  683.3 24.2 %copy-start.155 = (bf16[2,1024,256]{2,1,0:T(8,128)(2,1)S(1)}, bf16[2,1024,256]{2,1,0:T(8,128)(2,1)}, u32[]{:S(2)}) copy-start(bf16[2,1024,256]{2,1,0:T(8,128)(2,1)} %param.42) | copy-start | bytes 3145732
  726.7 17.2 all-to-all-start.4
  749.5 21.9 %copy-start.86 = (f32[8,4,608]{2,1,0:T(4,128)}, f32[8,4,608]{2,1,0:T(4,128)S(1)}, u32[]{:S(2)}) copy-start(f32[8,4,608]{2,1,0:T(4,128)S(1)} %get-tuple-element.1664) | copy-start | bytes 233476 | tf_op jit(solution)/shard_map/while
  805.3 21.9 %copy-start.86 = (f32[8,4,608]{2,1,0:T(4,128)}, f32[8,4,608]{2,1,0:T(4,128)S(1)}, u32[]{:S(2)}) copy-start(f32[8,4,608]{2,1,0:T(4,128)S(1)} %get-tuple-element.1664) | copy-start | bytes 233476 | tf_op jit(solution)/shard_map/while
  822.4 10.0 copy-start.77
  861.2 21.8 %copy-start.86 = (f32[8,4,608]{2,1,0:T(4,128)}, f32[8,4,608]{2,1,0:T(4,128)S(1)}, u32[]{:S(2)}) copy-start(f32[8,4,608]{2,1,0:T(4,128)S(1)} %get-tuple-element.1664) | copy-start | bytes 233476 | tf_op jit(solution)/shard_map/while
  917.1 21.9 %copy-start.86 = (f32[8,4,608]{2,1,0:T(4,128)}, f32[8,4,608]{2,1,0:T(4,128)S(1)}, u32[]{:S(2)}) copy-start(f32[8,4,608]{2,1,0:T(4,128)S(1)} %get-tuple-element.1664) | copy-start | bytes 233476 | tf_op jit(solution)/shard_map/while
  934.1 10.0 copy-start.77
  972.9 21.9 %copy-start.86 = (f32[8,4,608]{2,1,0:T(4,128)}, f32[8,4,608]{2,1,0:T(4,128)S(1)}, u32[]{:S(2)}) copy-start(f32[8,4,608]{2,1,0:T(4,128)S(1)} %get-tuple-element.1664) | copy-start | bytes 233476 | tf_op jit(solution)/shard_map/while
  989.9 10.0 copy-start.77
  1028.7 21.8 %copy-start.86 = (f32[8,4,608]{2,1,0:T(4,128)}, f32[8,4,608]{2,1,0:T(4,128)S(1)}, u32[]{:S(2)}) copy-start(f32[8,4,608]{2,1,0:T(4,128)S(1)} %get-tuple-element.1664) | copy-start | bytes 233476 | tf_op jit(solution)/shard_map/while
  1084.6 21.9 %copy-start.86 = (f32[8,4,608]{2,1,0:T(4,128)}, f32[8,4,608]{2,1,0:T(4,128)S(1)}, u32[]{:S(2)}) copy-start(f32[8,4,608]{2,1,0:T(4,128)S(1)} %get-tuple-element.1664) | copy-start | bytes 233476 | tf_op jit(solution)/shard_map/while
  1101.7 10.0 copy-start.77
  1140.5 21.9 %copy-start.86 = (f32[8,4,608]{2,1,0:T(4,128)}, f32[8,4,608]{2,1,0:T(4,128)S(1)}, u32[]{:S(2)}) copy-start(f32[8,4,608]{2,1,0:T(4,128)S(1)} %get-tuple-element.1664) | copy-start | bytes 233476 | tf_op jit(solution)/shard_map/while
  1157.6 10.0 copy-start.77
  1197.0 13.5 copy-start.109
  1197.0 44.7 %all-to-all-start.5 = ((bf16[8,608,3,128]{3,1,2,0:T(8,128)(2,1)}), bf16[8,608,3,128]{3,1,2,0:T(8,128)(2,1)}, u32[]{:S(2)}, u32[]{:S(2)}) async-start(bf16[8,608,3,128]{3,1,2,0:T(8,128)(2,1)} %get-tuple-element.607), calls=%async_computation.5 | async-start | bytes 7471104 | tf_op jit(solution)/shard_map/all_to_all | solution.py:291
  1213.9 35.6 %copy-start.152 = (f32[1,256]{1,0:T(1,128)}, f32[1,256]{1,0:T(1,128)S(1)}, u32[]{:S(2)}) copy-start(f32[1,256]{1,0:T(1,128)S(1)} %constant_dynamic-update-slice_fusion) | copy-start | bytes 3076
  1267.5 14.3 copy-start.23
  1267.6 10.3 copy-start.11
  1267.6 10.3 copy-start.66
  1267.6 10.3 copy-start.74
  1267.6 10.3 copy-start.118
  1267.6 10.3 copy-start.160
  1286.1 10.2 copy-start.151
  1286.1 10.7 copy-start.150
  1286.1 11.3 copy-start.137
  1286.1 11.9 copy-start.24
  1289.7 16.3 all-to-all-start.6
  1330.8 11.1 copy-start.81
  1388.8 11.1 copy-start.81
  1446.8 11.1 copy-start.81
  1504.8 11.1 copy-start.81
  1562.8 11.1 copy-start.81
  1620.9 11.1 copy-start.81
  1678.8 11.1 copy-start.81
  1736.8 11.1 copy-start.81
  1777.3 42.4 %all-to-all-start.7 = ((bf16[8,608,3,128]{3,1,2,0:T(8,128)(2,1)}), bf16[8,608,3,128]{3,1,2,0:T(8,128)(2,1)}, u32[]{:S(2)}, u32[]{:S(2)}) async-start(bf16[8,608,3,128]{3,1,2,0:T(8,128)(2,1)} %get-tuple-element.608), calls=%async_computation.7 | async-start | bytes 7471104 | tf_op jit(solution)/shard_map/all_to_all | solution.py:291
  1782.9 218.7 %all-reduce.4.cloned.1.call-start = ((), (), s32[]{:S(2)}) async-start(), calls=%async_computation.8 | async-start | bytes 12582912 | tf_op jit(solution)/shard_map/psum | solution.py:353
  1845.3 47.6 %copy-start.98 = (f32[4,608]{1,0:T(4,128)S(1)}, f32[4,608]{1,0:T(4,128)}, u32[]{:S(2)}) copy-start(f32[4,608]{1,0:T(4,128)} %copy-done.97) | copy-start | bytes 29188
  (377 other events, 1622.0 us)
Sparse Core Ops, SparseCore 0:
  1845.3 156.2 all-reduce.3
where the time goes:
time: 2030 us; the launch traced here: 2020 us
  local copies, waits for them, and re-layouts  799 us (39%)
  matrix products  453 us (22%)
  other arithmetic  375 us (18%)
  waiting for transfers between devices  225 us (11%)
  blocking collectives  103 us (5%)
  starting transfers between devices  35 us (2%)
    gather x16, local copies, waits for them, and re-layouts, group_forward(): neighbours_v = jnp.take(values_in, places, axis=0).astype(jnp.float32)  175 us
    gather x16, local copies, waits for them, and re-layouts, group_backward(): neighbours_v = jnp.take(values_in, places, axis=0).astype(jnp.float32)  175 us
    gather x16, local copies, waits for them, and re-layouts, group_backward(): back_near = jnp.take(grad_float, places[::-1], axis=0)  143 us
    psum x1, waiting for transfers between devices, local(): lax.psum((all_gain_a, all_shift_a, all_qkv, all_lepe_w, all_lepe_b, all_p...  103 us
    dot_general x16, matrix products, group_backward(): jnp.einsum('thd,uhd->htu', grad_heads, values_heads, preferred_element_ty...  84.2 us
    dot_general x32, matrix products, masked_scores(): jnp.einsum('thd,uhd->htu', queries, keys_in, preferred_element_type=jnp.f...  80.6 us
    dot_general x16, matrix products, group_backward(): jnp.einsum('htu,thd->uhd', probabilities, grad_heads, preferred_element_t...  71.3 us
    dot_general x16, matrix products, group_forward(): jnp.einsum('htu,uhd->thd', probabilities, values_in.reshape(TOK_IMG, grou...  71 us
  transfers between devices with their start and end apart: 8, of which 7 were waited for; matrix products, arithmetic and copies ran while one was open for 3% of the time, Pallas kernels for 0%

commit v1 on v0

v1 whole, which is shorter than its diff:
```python
from functools import partial
import math

import jax
import jax.numpy as jnp
import numpy as np
from jax import lax
from jax.experimental import pallas as pl
from jax.experimental.pallas import tpu as pltpu
from jax.sharding import PartitionSpec as P

HEADS_GROUP = 4
HEAD_DIM = 32
SW = 7
BIG = 14
SMALL = 6
BIG_CROPS = 2
SMALL_CROPS = 6
GROUP = 128
EPSILON = 1e-05

BIG_ROWS = BIG * 16
WIN = SW * 16
SMALL_ROWS = SMALL * 8
SMALL_BASE = BIG_CROPS * BIG_ROWS
ROWS = SMALL_BASE + SMALL_CROPS * SMALL_ROWS
CHUNK = ROWS // 2

SCALE = HEAD_DIM**-0.5
LOG2E = math.log2(math.e)
NEG = -1e30

bf16 = jnp.bfloat16
f32 = jnp.float32

NN = (((1,), (0,)), ((), ()))
NT = (((1,), (1,)), ((), ()))
TN = (((0,), (0,)), ((), ()))


def mm(a, b, dims=NN):
    return lax.dot_general(a, b, dims, preferred_element_type=f32)


def iota(shape, dim):
    return lax.broadcasted_iota(jnp.int32, shape, dim)


def to_vertical(x):
    x4 = x.reshape(BIG, 2, 8, x.shape[1])
    return jnp.concatenate([x4[:, 0].reshape(WIN, -1), x4[:, 1].reshape(WIN, -1)], axis=0)


def from_vertical(y):
    y4 = y.reshape(2, BIG, 8, y.shape[1])
    return jnp.stack([y4[0], y4[1]], axis=1).reshape(BIG_ROWS, -1)


def real_big():
    sub = iota((BIG_ROWS, GROUP), 0) % 16
    return ((sub != 0) & (sub != 15)).astype(f32)


def real_small(rows):
    return ((iota((rows, GROUP), 0) % 8) < SMALL).astype(f32)


def partial_rows(x):
    return jnp.sum(x.reshape(x.shape[0] // 8, 8, x.shape[1]), axis=0)


def head_mask(h):
    lane = iota((1, GROUP), 1)
    return ((lane >= h * HEAD_DIM) & (lane < (h + 1) * HEAD_DIM)).astype(f32)


def block_heads(x, keys):
    rows = x.shape[0]
    parts = []
    for h in range(HEADS_GROUP):
        part = x * head_mask(h).astype(x.dtype)
        parts.append(part)
        if keys > rows:
            parts.append(jnp.zeros((keys - rows, GROUP), x.dtype))
    return jnp.concatenate(parts, axis=0)


def ones_heads(keys):
    row_head = iota((HEADS_GROUP * keys, GROUP), 0) // keys
    lane_head = iota((HEADS_GROUP * keys, GROUP), 1) // HEAD_DIM
    return (row_head == lane_head).astype(f32).astype(bf16)


def sum_heads(x, keys, rows):
    total = None
    for h in range(HEADS_GROUP):
        part = x[h * keys : h * keys + rows] * head_mask(h)
        total = part if total is None else total + part
    return total


def kernel(
    crop_side,
    tokens,
    cotangent,
    ln1_gain,
    ln1_bias,
    qkv_w,
    lepe_w,
    lepe_b,
    proj_w,
    proj_b,
    ln2_gain,
    ln2_bias,
    fc1_w,
    fc1_b,
    fc2_w,
    fc2_b,
    out,
    input_grad,
    g_gain1,
    g_bias1,
    g_qkv,
    g_lepe_w,
    g_lepe_b,
    g_proj,
    g_proj_b,
    g_gain2,
    g_bias2,
    g_fc1,
    g_fc1_b,
    g_fc2,
    g_fc2_b,
    starts,
    stage,
    x_s,
    mid_s,
    e_s,
    n1_s,
    r1_s,
    a_s,
    q_s,
    k_s,
    v_s,
    eb_s,
    es_s,
    oat_s,
    rdn_s,
    o_s,
    n2_s,
    r2_s,
    m_s,
    g_s,
    gp_s,
    df_s,
    do_s,
    dqkv_s,
    lepb,
    leps,
    onesb,
    oness,
    vec,
    acc_gain1,
    acc_bias1,
    acc_lepe,
    acc_lepe_b,
    acc_proj_b,
    acc_gain2,
    acc_bias2,
    acc_fc1_b,
    acc_fc2_b,
):
    image = pl.program_id(0)
    images = pl.num_programs(0)
    layers = qkv_w.shape[0]
    dim = tokens.shape[2]
    tok = tokens.shape[1]
    crops = crop_side.shape[1]
    ff = fc1_w.shape[2]
    halves = dim // GROUP

    big_accs = (g_qkv, g_proj, g_fc1, g_fc2)
    small_accs = (
        acc_gain1,
        acc_bias1,
        acc_lepe,
        acc_lepe_b,
        acc_proj_b,
        acc_gain2,
        acc_bias2,
        acc_fc1_b,
        acc_fc2_b,
    )

    @pl.when(image == 0)
    def _():
        for ref in big_accs + small_accs:
            ref[...] = jnp.zeros(ref.shape, f32)
        lepb[...] = jnp.zeros(lepb.shape, f32)
        leps[...] = jnp.zeros(leps.shape, f32)
        stage[...] = jnp.zeros(stage.shape, f32)
        onesb[...] = ones_heads(GROUP)
        oness[...] = ones_heads(64)
        for l in range(layers):
            for i, ref in enumerate(
                (ln1_gain, ln1_bias, lepe_b, proj_b, ln2_gain, ln2_bias, fc1_b, fc2_b)
            ):
                vec[l, i : i + 1, : ref.shape[1]] = ref[l : l + 1, :]

    def place(j, carry):
        start, n_big, n_small = carry
        side = crop_side[image, j]
        is_big = side == BIG
        slot = jnp.where(is_big, n_big, BIG_CROPS + n_small)
        starts[slot] = start
        big_add = is_big.astype(jnp.int32)
        return (start + side * side, n_big + big_add, n_small + 1 - big_add)

    zero = jnp.int32(0)
    lax.fori_loop(0, crops, place, (zero, zero, zero))

    keep_lo = (iota((8, GROUP), 0) != 0).astype(f32)
    keep_hi = (iota((8, GROUP), 0) != 7).astype(f32)
    keep_small = (iota((8, GROUP), 0) < SMALL).astype(f32)

    def ingest(source, target):
        for half in range(halves):
            stage[half, 8 : 8 + tok, :] = source[0, :, half * GROUP : (half + 1) * GROUP].astype(f32)
        for c in range(BIG_CROPS):
            start = starts[c] + 7
            for r in range(BIG):
                for half in range(halves):
                    lanes = slice(half * GROUP, (half + 1) * GROUP)
                    base = c * BIG_ROWS + r * 16
                    lo = stage[half, pl.ds(start + r * BIG, 8), :]
                    hi = stage[half, pl.ds(start + r * BIG + 8, 8), :]
                    target[base : base + 8, lanes] = lo * keep_lo
                    target[base + 8 : base + 16, lanes] = hi * keep_hi
        for c in range(SMALL_CROPS):
            start = starts[BIG_CROPS + c] + 8
            for r in range(SMALL):
                for half in range(halves):
                    lanes = slice(half * GROUP, (half + 1) * GROUP)
                    base = SMALL_BASE + c * SMALL_ROWS + r * 8
                    lo = stage[half, pl.ds(start + r * SMALL, 8), :]
                    target[base : base + 8, lanes] = lo * keep_small

    def put(half, at, value, keep):
        old = stage[half, pl.ds(at, 8), :]
        stage[half, pl.ds(at, 8), :] = jnp.where(keep > 0, value, old)

    def emit(source, target):
        for c in range(BIG_CROPS):
            start = starts[c] + 7
            for r in range(BIG):
                for half in range(halves):
                    lanes = slice(half * GROUP, (half + 1) * GROUP)
                    base = c * BIG_ROWS + r * 16
                    put(half, start + r * BIG, source[base : base + 8, lanes], keep_lo)
                    put(half, start + r * BIG + 8, source[base + 8 : base + 16, lanes], keep_hi)
        for c in range(SMALL_CROPS):
            start = starts[BIG_CROPS + c] + 8
            for r in range(SMALL):
                for half in range(halves):
                    lanes = slice(half * GROUP, (half + 1) * GROUP)
                    base = SMALL_BASE + c * SMALL_ROWS + r * 8
                    put(half, start + r * SMALL, source[base : base + 8, lanes], keep_small)
        for half in range(halves):
            target[0, :, half * GROUP : (half + 1) * GROUP] = stage[half, 8 : 8 + tok, :].astype(
                target.dtype
            )

    def norm_stats(x):
        center = x - jnp.mean(x, axis=1, keepdims=True)
        r = lax.rsqrt(jnp.mean(center * center, axis=1, keepdims=True) + EPSILON)
        return center * r, r

    def project(l, base, rows, big):
        rows_at = pl.ds(base, rows)
        n, r = norm_stats(x_s[rows_at, :])
        n1_s[l, rows_at, :] = n
        r1_s[l, rows_at, :] = jnp.broadcast_to(r, (rows, GROUP))
        a = (n * vec[l, 0:1, :dim] + vec[l, 1:2, :dim]).astype(bf16)
        a_s[l, rows_at, :] = a
        qkv = mm(a, qkv_w[l])
        real = real_big() if big else real_small(rows)
        for grp in range(2):
            cols = [slice(s * dim + grp * GROUP, s * dim + (grp + 1) * GROUP) for s in range(3)]
            q = qkv[:, cols[0]] * (SCALE * LOG2E)
            k = qkv[:, cols[1]]
            v = qkv[:, cols[2]] * real
            if big and grp == 1:
                q, k, v = to_vertical(q), to_vertical(k), to_vertical(v)
            lanes = slice(grp * GROUP, (grp + 1) * GROUP)
            q_s[l, rows_at, lanes] = q.astype(bf16)
            k_s[l, rows_at, lanes] = k.astype(bf16)
            v_s[l, rows_at, lanes] = v.astype(bf16)

    def pad_row(grp, w):
        u = iota((1, HEADS_GROUP * GROUP), 1) % GROUP
        if grp == 0:
            bad = (u % 16 == 0) | (u % 16 == 15)
        elif w == 0:
            bad = u % 8 == 0
        else:
            bad = u % 8 == 7
        return jnp.where(bad | (u >= WIN), NEG, 0.0).astype(f32)

    def pad_row_small():
        u = iota((1, HEADS_GROUP * 64), 1) % 64
        return jnp.where((u % 8 >= SMALL) | (u >= SMALL_ROWS), NEG, 0.0).astype(f32)

    def shifted(buf, idx, margin, stride, rows):
        return [buf[idx, pl.ds(margin - stride + b, rows + 2 * stride), :] for b in (-1, 0, 1)]

    def conv(views, stride, rows, weights, flip):
        total = None
        for a in range(3):
            for b in range(3):
                k = 3 * a + b
                wk = weights[8 - k : 9 - k] if flip else weights[k : k + 1]
                term = views[b][a * stride : a * stride + rows] * wk
                total = term if total is None else total + term
        return total

    def windows_big(c):
        for grp in range(2):
            for w in range(2):
                yield grp, w, c * BIG_ROWS + w * WIN

    def attend_big(l, c):
        items = list(windows_big(c))
        scores = []
        for grp, w, base in items:
            lanes = slice(grp * GROUP, (grp + 1) * GROUP)
            q = q_s[l, pl.ds(base, WIN), lanes]
            kb = block_heads(k_s[l, pl.ds(base, WIN), lanes], GROUP)
            scores.append(mm(q, kb, NT) + pad_row(grp, w))
        for i, (grp, w, base) in enumerate(items):
            parts = []
            for h in range(HEADS_GROUP):
                s = scores[i][:, h * GROUP : (h + 1) * GROUP]
                parts.append(jnp.exp2(s - jnp.max(s, axis=1, keepdims=True)).astype(bf16))
            eb_s[l, 4 * c + 2 * grp + w] = jnp.concatenate(parts, axis=1)
        outs = []
        for i, (grp, w, base) in enumerate(items):
            lanes = slice(grp * GROUP, (grp + 1) * GROUP)
            v = v_s[l, pl.ds(base, WIN), lanes]
            vo = jnp.concatenate([block_heads(v, GROUP), onesb[...]], axis=1)
            both = mm(eb_s[l, 4 * c + 2 * grp + w], vo)
            rden = 1.0 / both[:, GROUP:]
            oat = both[:, :GROUP] * rden
            rdn_s[l, pl.ds(base, WIN), lanes] = rden
            oat_s[l, pl.ds(base, WIN), lanes] = oat
            stride = 16 if grp == 0 else 8
            lepb[i, pl.ds(24, WIN), :] = v.astype(f32)
            views = shifted(lepb, i, 24, stride, WIN)
            near = conv(views, stride, WIN, lepe_w[l, :, lanes], False)
            outs.append(oat + near + vec[l, 2:3, lanes])
        rows_at = pl.ds(c * BIG_ROWS, BIG_ROWS)
        o_s[l, rows_at, :GROUP] = jnp.concatenate(outs[:2], axis=0).astype(bf16)
        o_s[l, rows_at, GROUP:] = from_vertical(jnp.concatenate(outs[2:], axis=0)).astype(bf16)

    def attend_small(l, c0, count):
        items = [
            (grp, c0 + c, SMALL_BASE + (c0 + c) * SMALL_ROWS, 2 * c + grp)
            for c in range(count)
            for grp in range(2)
        ]
        low = iota((SMALL_ROWS, GROUP), 1) < 64
        scores = []
        for grp, c, base, i in items:
            lanes = slice(grp * GROUP, (grp + 1) * GROUP)
            q = q_s[l, pl.ds(base, SMALL_ROWS), lanes]
            kb = block_heads(k_s[l, pl.ds(base, SMALL_ROWS), lanes], 64)
            scores.append(mm(q, kb, NT) + pad_row_small())
        for j, (grp, c, base, i) in enumerate(items):
            parts = []
            for t in range(2):
                s = scores[j][:, t * GROUP : (t + 1) * GROUP]
                top_lo = jnp.max(jnp.where(low, s, 2 * NEG), axis=1, keepdims=True)
                top_hi = jnp.max(jnp.where(low, 2 * NEG, s), axis=1, keepdims=True)
                parts.append(jnp.exp2(s - jnp.where(low, top_lo, top_hi)).astype(bf16))
            es_s[l, 2 * c + grp] = jnp.concatenate(parts, axis=1)
        for grp, c, base, i in items:
            lanes = slice(grp * GROUP, (grp + 1) * GROUP)
            v = v_s[l, pl.ds(base, SMALL_ROWS), lanes]
            vo = jnp.concatenate([block_heads(v, 64), oness[...]], axis=1)
            both = mm(es_s[l, 2 * c + grp], vo)
            rden = 1.0 / both[:, GROUP:]
            oat = both[:, :GROUP] * rden
            rdn_s[l, pl.ds(base, SMALL_ROWS), lanes] = rden
            oat_s[l, pl.ds(base, SMALL_ROWS), lanes] = oat
            leps[i, pl.ds(16, SMALL_ROWS), :] = v.astype(f32)
            views = shifted(leps, i, 16, 8, SMALL_ROWS)
            near = conv(views, 8, SMALL_ROWS, lepe_w[l, :, lanes], False)
            o_s[l, pl.ds(base, SMALL_ROWS), lanes] = (oat + near + vec[l, 2:3, lanes]).astype(
                bf16
            )

    def feed(l, base):
        rows_at = pl.ds(base, CHUNK)
        mid = x_s[rows_at, :] + mm(o_s[l, rows_at, :], proj_w[l]) + vec[l, 3:4, :dim]
        n, r = norm_stats(mid)
        n2_s[l, rows_at, :] = n
        r2_s[l, rows_at, :] = jnp.broadcast_to(r, (CHUNK, GROUP))
        m = (n * vec[l, 4:5, :dim] + vec[l, 5:6, :dim]).astype(bf16)
        m_s[l, rows_at, :] = m
        total = mid + vec[l, 7:8, :dim]
        step = 256
        for j in range(ff // step):
            cols = slice(j * step, (j + 1) * step)
            f = mm(m, fc1_w[l, :, cols]) + vec[l, 6:7, cols]
            phi = 0.5 * lax.erf(f * np.float32(math.sqrt(0.5))) + 0.5
            dens = jnp.exp2(f * f * np.float32(-0.5 * LOG2E)) * np.float32(
                1.0 / math.sqrt(2.0 * math.pi)
            )
            g = (f * phi).astype(bf16)
            g_s[l, rows_at, cols] = g
            gp_s[l, rows_at, cols] = (phi + f * dens).astype(bf16)
            total = total + mm(g, fc2_w[l, cols, :])
        x_s[rows_at, :] = total

    def norm_back(dm, n, r, gain):
        dn = dm * gain
        mean_one = jnp.mean(dn, axis=1, keepdims=True)
        mean_two = jnp.mean(dn * n, axis=1, keepdims=True)
        rb = jnp.concatenate([r] * halves, axis=1)
        return rb * (dn - mean_one - n * mean_two)

    def feed_back(l, base):
        rows_at = pl.ds(base, CHUNK)
        e = e_s[rows_at, :]
        dz = e.astype(bf16)
        acc_fc2_b[l] += partial_rows(dz.astype(f32))
        dm = None
        step = 256
        for j in range(ff // step):
            cols = slice(j * step, (j + 1) * step)
            dg = mm(dz, fc2_w[l, cols, :], NT)
            df = (dg * gp_s[l, rows_at, cols].astype(f32)).astype(bf16)
            df_s[rows_at, cols] = df
            acc_fc1_b[l, :, cols] += partial_rows(df.astype(f32))
            part = mm(df, fc1_w[l, :, cols], NT)
            dm = part if dm is None else dm + part
        n = n2_s[l, rows_at, :]
        acc_gain2[l] += partial_rows(dm * n)
        acc_bias2[l] += partial_rows(dm)
        dmid = e + norm_back(dm, n, r2_s[l, rows_at, :], vec[l, 4:5, :dim])
        mid_s[rows_at, :] = dmid
        dy = dmid.astype(bf16)
        acc_proj_b[l] += partial_rows(dy.astype(f32))
        do_s[rows_at, :] = mm(dy, proj_w[l], NT).astype(bf16).astype(f32)

    def lepe_back(l, buf, idx, margin, stride, rows, lanes, v):
        views = [buf[idx, pl.ds(margin - stride + b, rows + 2 * stride), :] for b in (-1, 0, 1)]
        vf = v.astype(f32)
        for k in range(9):
            a, b = divmod(8 - k, 3)
            acc_lepe[l, k, :, lanes] += partial_rows(views[b][a * stride : a * stride + rows] * vf)
        acc_lepe_b[l, :, lanes] += partial_rows(views[1][stride : stride + rows])
        return conv(views, stride, rows, lepe_w[l, :, lanes], True)

    def attend_back(l, group_items, rows, keys, buf, margin, strides, e_ref, ones, unit):
        grads = []
        kbs = []
        ds_all = []
        dop_all = []
        for grp, base, e_at, lep_at, do in group_items:
            lanes = slice(grp * GROUP, (grp + 1) * GROUP)
            rows_at = pl.ds(base, rows)
            buf[lep_at, pl.ds(margin, rows), :] = do
            dop = do * rdn_s[l, rows_at, lanes]
            tail = -(dop * oat_s[l, rows_at, lanes])
            dop_all.append(dop.astype(bf16))
            left = jnp.concatenate([dop.astype(bf16), tail.astype(bf16)], axis=1)
            vo = jnp.concatenate([block_heads(v_s[l, rows_at, lanes], keys), ones[...]], axis=1)
            x = mm(left, vo, NT)
            ds_all.append((e_ref[l, e_at].astype(f32) * x).astype(bf16))
        for i, (grp, base, e_at, lep_at, do) in enumerate(group_items):
            lanes = slice(grp * GROUP, (grp + 1) * GROUP)
            kb = block_heads(k_s[l, pl.ds(base, rows), lanes], keys)
            grads.append([mm(ds_all[i], kb) * SCALE])
        zero_block = jnp.zeros((rows, GROUP), bf16)
        for i in range(0, len(group_items), 2):
            pair = group_items[i : i + 2]

            def spread(first, second):
                return jnp.concatenate(
                    [
                        jnp.concatenate([first, zero_block], axis=1),
                        jnp.concatenate([zero_block, second], axis=1),
                    ],
                    axis=0,
                )

            qs = [q_s[l, pl.ds(it[1], rows), it[0] * GROUP : (it[0] + 1) * GROUP] for it in pair]
            dk = mm(jnp.concatenate(ds_all[i : i + 2], axis=0), spread(*qs), TN)
            es = jnp.concatenate([e_ref[l, it[2]] for it in pair], axis=0)
            dv = mm(es, spread(*dop_all[i : i + 2]), TN)
            for j, (grp, base, e_at, lep_at, do) in enumerate(pair):
                lanes = slice(grp * GROUP, (grp + 1) * GROUP)
                cols = slice(j * GROUP, (j + 1) * GROUP)
                near = lepe_back(
                    l, buf, lep_at, margin, strides[grp], rows, lanes, v_s[l, pl.ds(base, rows), lanes]
                )
                grads[i + j].append(sum_heads(dk[:, cols], keys, rows) * (1.0 / LOG2E))
                grads[i + j].append(sum_heads(dv[:, cols], keys, rows) + near)
        return grads

    def attend_back_big(l, c):
        rows_at = pl.ds(c * BIG_ROWS, BIG_ROWS)
        do_h = do_s[rows_at, :GROUP]
        do_v = to_vertical(do_s[rows_at, GROUP:])
        items = []
        for i, (grp, w, base) in enumerate(windows_big(c)):
            do = (do_h if grp == 0 else do_v)[w * WIN : (w + 1) * WIN]
            items.append((grp, base, 4 * c + 2 * grp + w, i, do))
        grads = attend_back(l, items, WIN, GROUP, lepb, 24, (16, 8), eb_s, onesb, None)
        real = real_big()
        for s in range(3):
            left = jnp.concatenate([grads[0][s], grads[1][s]], axis=0)
            right = from_vertical(jnp.concatenate([grads[2][s], grads[3][s]], axis=0))
            if s == 2:
                left, right = left * real, right * real
            dqkv_s[rows_at, s * dim : s * dim + GROUP] = left.astype(bf16)
            dqkv_s[rows_at, s * dim + GROUP : (s + 1) * dim] = right.astype(bf16)

    def attend_back_small(l, c0, count):
        items = []
        for grp in range(2):
            for c in range(count):
                base = SMALL_BASE + (c0 + c) * SMALL_ROWS
                do = do_s[pl.ds(base, SMALL_ROWS), grp * GROUP : (grp + 1) * GROUP]
                items.append((grp, base, 2 * (c0 + c) + grp, 2 * c + grp, do))
        grads = attend_back(l, items, SMALL_ROWS, 64, leps, 16, (8, 8), es_s, oness, None)
        real = real_small(SMALL_ROWS)
        for (grp, base, e_at, lep_at, do), grad in zip(items, grads):
            for s in range(3):
                value = grad[s] * real if s == 2 else grad[s]
                at = s * dim + grp * GROUP
                dqkv_s[pl.ds(base, SMALL_ROWS), at : at + GROUP] = value.astype(bf16)

    def project_back(l, base):
        rows_at = pl.ds(base, CHUNK)
        da = mm(dqkv_s[rows_at, :], qkv_w[l], NT)
        n = n1_s[l, rows_at, :]
        acc_gain1[l] += partial_rows(da * n)
        acc_bias1[l] += partial_rows(da)
        e_s[rows_at, :] = mid_s[rows_at, :] + norm_back(
            da, n, r1_s[l, rows_at, :], vec[l, 0:1, :dim]
        )

    def loop(count, body):
        def step(i, carry):
            body(i)
            return carry

        lax.fori_loop(0, count, step, 0)

    ingest(tokens, x_s)

    def forward_layer(l):
        loop(BIG_CROPS, lambda c: project(l, pl.multiple_of(c * BIG_ROWS, 16), BIG_ROWS, True))
        project(l, SMALL_BASE, ROWS - SMALL_BASE, False)
        loop(BIG_CROPS, lambda c: attend_big(l, c))
        loop(SMALL_CROPS // 2, lambda c: attend_small(l, 2 * c, 2))
        loop(2, lambda c: feed(l, pl.multiple_of(c * CHUNK, 16)))

    loop(layers, forward_layer)
    emit(x_s, out)
    ingest(cotangent, e_s)

    def backward_layer(step):
        l = layers - 1 - step
        loop(2, lambda c: feed_back(l, pl.multiple_of(c * CHUNK, 16)))
        dz = e_s[...].astype(bf16)
        g_fc2[l] += mm(g_s[l], dz, TN)
        g_fc1[l] += mm(m_s[l], df_s[...], TN)
        g_proj[l] += mm(o_s[l], mid_s[...].astype(bf16), TN)
        loop(BIG_CROPS, lambda c: attend_back_big(l, c))
        loop(SMALL_CROPS // 2, lambda c: attend_back_small(l, 2 * c, 2))
        g_qkv[l] += mm(a_s[l], dqkv_s[...], TN)
        loop(2, lambda c: project_back(l, pl.multiple_of(c * CHUNK, 16)))

    loop(layers, backward_layer)
    emit(e_s, input_grad)

    @pl.when(image == images - 1)
    def _():
        for acc, target in (
            (acc_gain1, g_gain1),
            (acc_bias1, g_bias1),
            (acc_lepe_b, g_lepe_b),
            (acc_proj_b, g_proj_b),
            (acc_gain2, g_gain2),
            (acc_bias2, g_bias2),
            (acc_fc1_b, g_fc1_b),
            (acc_fc2_b, g_fc2_b),
        ):
            target[...] = jnp.sum(acc[...], axis=1)
        g_lepe_w[...] = jnp.sum(acc_lepe[...], axis=2)


def local(
    tokens,
    crop_side,
    cotangent,
    ln1_gain,
    ln1_bias,
    qkv_weight,
    lepe_weight,
    lepe_bias,
    proj_weight,
    proj_bias,
    ln2_gain,
    ln2_bias,
    fc1_weight,
    fc1_bias,
    fc2_weight,
    fc2_bias,
):
    images, tok, dim = tokens.shape
    layers = qkv_weight.shape[0]
    ff = fc1_weight.shape[2]
    weights = (
        ln1_gain,
        ln1_bias,
        qkv_weight,
        lepe_weight,
        lepe_bias,
        proj_weight,
        proj_bias,
        ln2_gain,
        ln2_bias,
        fc1_weight,
        fc1_bias,
        fc2_weight,
        fc2_bias,
    )
    block = pl.BlockSpec((1, tok, dim), lambda i: (i, 0, 0))
    whole = pl.BlockSpec(memory_space=pltpu.VMEM)
    results = pl.pallas_call(
        kernel,
        grid=(images,),
        out_shape=[
            jax.ShapeDtypeStruct(tokens.shape, bf16),
            jax.ShapeDtypeStruct(tokens.shape, f32),
        ]
        + [jax.ShapeDtypeStruct(w.shape, f32) for w in weights],
        in_specs=[pl.BlockSpec(memory_space=pltpu.SMEM), block, block] + [whole] * len(weights),
        out_specs=[block, block] + [whole] * len(weights),
        scratch_shapes=[
            pltpu.SMEM((BIG_CROPS + SMALL_CROPS,), jnp.int32),
            pltpu.VMEM((dim // GROUP, tok + 16, GROUP), f32),
            pltpu.VMEM((ROWS, dim), f32),
            pltpu.VMEM((ROWS, dim), f32),
            pltpu.VMEM((ROWS, dim), f32),
            pltpu.VMEM((layers, ROWS, dim), f32),
            pltpu.VMEM((layers, ROWS, GROUP), f32),
            pltpu.VMEM((layers, ROWS, dim), bf16),
            pltpu.VMEM((layers, ROWS, dim), bf16),
            pltpu.VMEM((layers, ROWS, dim), bf16),
            pltpu.VMEM((layers, ROWS, dim), bf16),
            pltpu.VMEM((layers, 4 * BIG_CROPS, WIN, 4 * GROUP), bf16),
            pltpu.VMEM((layers, 2 * SMALL_CROPS, SMALL_ROWS, 2 * GROUP), bf16),
            pltpu.VMEM((layers, ROWS, dim), f32),
            pltpu.VMEM((layers, ROWS, dim), f32),
            pltpu.VMEM((layers, ROWS, dim), bf16),
            pltpu.VMEM((layers, ROWS, dim), f32),
            pltpu.VMEM((layers, ROWS, GROUP), f32),
            pltpu.VMEM((layers, ROWS, dim), bf16),
            pltpu.VMEM((layers, ROWS, ff), bf16),
            pltpu.VMEM((layers, ROWS, ff), bf16),
            pltpu.VMEM((ROWS, ff), bf16),
            pltpu.VMEM((ROWS, dim), f32),
            pltpu.VMEM((ROWS, 3 * dim), bf16),
            pltpu.VMEM((4, WIN + 48, GROUP), f32),
            pltpu.VMEM((4, SMALL_ROWS + 32, GROUP), f32),
            pltpu.VMEM((4 * GROUP, GROUP), bf16),
            pltpu.VMEM((4 * 64, GROUP), bf16),
            pltpu.VMEM((layers, 8, ff), f32),
            pltpu.VMEM((layers, 8, dim), f32),
            pltpu.VMEM((layers, 8, dim), f32),
            pltpu.VMEM((layers, 9, 8, dim), f32),
            pltpu.VMEM((layers, 8, dim), f32),
            pltpu.VMEM((layers, 8, dim), f32),
            pltpu.VMEM((layers, 8, dim), f32),
            pltpu.VMEM((layers, 8, dim), f32),
            pltpu.VMEM((layers, 8, ff), f32),
            pltpu.VMEM((layers, 8, dim), f32),
        ],
        compiler_params=pltpu.CompilerParams(
            dimension_semantics=("arbitrary",), vmem_limit_bytes=62 * 1024 * 1024
        ),
    )(crop_side, tokens, cotangent, *weights)
    grads = lax.psum(tuple(results[2:]), ("dp", "head"))
    factor = 1.0 / math.sqrt(lax.axis_size("dp") * lax.axis_size("head") * images * tok)
    return (results[0], results[1]) + tuple(g * factor for g in grads)


def solution(mesh):
    sharded = P(("dp", "head"), None, None)
    return jax.shard_map(
        local,
        mesh=mesh,
        in_specs=(sharded, P(("dp", "head"), None), sharded) + (P(),) * 13,
        out_specs=(sharded, sharded) + (P(),) * 13,
        check_vma=False,
    )
```

time: 2030 us -> 320 us (0.16)
  local copies, waits for them, and re-layouts: 799 us -> 3.12 us
  matrix products: 453 us -> 0 us
  other arithmetic: 375 us -> 9.83 us
  Pallas kernels: 0 us -> 136 us
  waiting for transfers between devices: 225 us -> 113 us
  blocking collectives: 103 us -> 43.8 us
  starting transfers between devices: 35 us -> 0.04 us
    gather x48 -> x0, local copies, waits for them, and re-layouts: 492 us -> none  [the longest x16 175 us: group_forward(): neighbours_v = jnp.take(values_in, places, axis=0).astype(jnp.float32)]
    dot_general x136 -> x0, matrix products: 453 us -> none  [the longest x16 84.2 us: group_backward(): jnp.einsum('thd,uhd->htu', grad_heads, values_heads, preferred_element_ty...]
    reduce_sum x160 -> x0, other arithmetic: 175 us -> none  [the longest x16 38.2 us: group_backward(): jnp.sum(lepe_w[:, None, :] * back_near * usable[::-1][:, :, None], axis=0)]
    pallas_call x0 -> x1, Pallas kernels: none -> 136 us  [local(): pl.pallas_call(kernel, grid=(images,), out_shape=[jax.ShapeDtypeStruct(to...]
    all_to_all x7 -> x0, waiting for transfers between devices: 123 us -> none  [the longest x2 52.9 us: local(): lax.all_to_all(shortened(grad_packed), 'head', split_axis=0, concat_axis=...]
    convert_element_type x66 -> x0, other arithmetic: 93.3 us -> none  [the longest x2 48.2 us: local(): active = gelu_exact(hidden).astype(jnp.bfloat16)]
    another operation x110 -> x0, local copies, waits for them, and re-layouts: 67.8 us -> none  [the longest x32 54.5 us: group_backward(): jnp.stack([grad_queries.reshape(TOK_IMG, group_width), grad_keys.reshape(...]
    all_to_all x12 -> x0, local copies, waits for them, and re-layouts: 55.3 us -> none  [the longest x4 21.8 us: local(): lax.all_to_all(packed, 'head', split_axis=3, concat_axis=0, tiled=True)]
  transfers between devices with their start and end apart: 8 -> 1, of which waited for: 7 -> 1; matrix products, arithmetic and copies ran while one was open for 3% -> 1% of each run, Pallas kernels for 0% -> 0%
where the time goes in v1:
time: 320 us
  Pallas kernels  136 us (42%)
  waiting for transfers between devices  113 us (35%)
  blocking collectives  43.8 us (14%)
  between operations  14.2 us (4%)
  other arithmetic  9.83 us (3%)
    pallas_call x1, Pallas kernels, local(): pl.pallas_call(kernel, grid=(images,), out_shape=[jax.ShapeDtypeStruct(to...  136 us
    psum x1, waiting for transfers between devices, local(): grads = lax.psum(tuple(results[2:]), ('dp', 'head'))  113 us
    psum x1, blocking collectives, local(): grads = lax.psum(tuple(results[2:]), ('dp', 'head'))  43.8 us
    mul x10, other arithmetic, local(): return (results[0], results[1]) + tuple((g * factor for g in grads))  9.83 us
  transfers between devices with their start and end apart: 1, of which 1 were waited for; matrix products, arithmetic and copies ran while one was open for 1% of the time, Pallas kernels for 0%

profile of v1, /device:TPU:0, one launch (start us, length us, event | category | flops | bytes accessed | tf_op | source)
XLA Modules:
  0.0 319.8 jit_solution(12391958435820508553)
XLA Ops:
  7.2 0.0 all-reduce.4.cloned.1.call-start
  7.2 1.3 copy.31.lepe_w
  8.6 136.2 %shard_map.271 = (bf16[4,608,256]{2,1,0:T(8,128)(2,1)}, f32[4,608,256]{2,1,0:T(8,128)}, f32[2,256]{1,0:T(2,128)}, f32[2,256]{1,0:T(2,128)}, f32[2,256,768]{2,1,0...) custom-call(s32[4,8]{1,0:T(4,128)} %crop_side.1, ...), custom_call_target="tpu_custom_call" | custom-call | tf_op jit(solution)/shard_map/pallas_call | solution.py:643
  144.8 0.0 copy-start.3
  144.8 0.0 copy-start.4
  144.8 0.0 copy-start.5
  144.8 0.0 copy-start.6
  144.8 0.0 copy-start.7
  144.8 0.0 copy-start.8
  144.9 0.0 copy-start.9
  144.9 0.0 copy-start.10
  144.9 0.0 copy-start.11
  144.9 0.0 all-reduce.4.cloned.1.call-update
  144.9 0.6 copy-done.3
  145.6 0.0 copy-done.4
  145.6 0.0 copy-done.5
  145.6 0.0 copy-done.6
  145.6 0.0 copy-done.7
  145.6 0.0 copy-done.8
  145.6 0.0 copy-done.9
  145.6 0.0 copy-done.10
  145.6 0.0 copy-done.11
  145.6 43.8 %all-reduce = (f32[2,256]{1,0:T(2,128)S(1)}, f32[2,256]{1,0:T(2,128)S(1)}, f32[2,9,256]{2,1,0:T(8,128)S(1)}, f32[2,256]{1,0:T(2,128)S(1)}, f32[2,256]{1,0:T(2,12...) all-reduce(f32[2,256]{1,0:T(2,128)S(1)} %copy-done.5, ...), channel_id=1, replica_groups=mesh['dp'=16,'head'=2] {'dp','head'}, use_global_device_ids=true, to_apply=%region_0.0 | all-reduce | flops 10240 | bytes 81920 | tf_op jit(solution)/shard_map/psum | solution.py:697
  189.4 0.6 copy.32
  190.1 0.6 broadcast_multiply_fusion.12
  190.6 0.6 broadcast_multiply_fusion.6
  191.2 0.6 broadcast_multiply_fusion.8
  191.8 0.6 broadcast_multiply_fusion.10
  192.4 0.6 broadcast_multiply_fusion.5
  193.0 112.5 %all-reduce.4.cloned.1.call-done = (f32[2,256,768]{2,1,0:T(8,128)}, f32[2,256,256]{2,1,0:T(8,128)}, f32[2,256,1024]{2,1,0:T(8,128)}, f32[2,1024,256]{2,1,0:T(8,128)}) async-done(((f32[2,256,768]{2,1,0:T(8,128)}, f32[2,256,256]{2,1,0:T(8,128)}, f32[2,256,1024]{2,1,0:T(8,128)}, f32[2,1024,256]{2,1,0:T(8,128)}), (f32[2,256,768]{2,1,0:T(8,128)}, f32[2,256,256]{2,1,0:T(8,128)}, f32[2,256,1024]{2,1,0:T(8,128)}, ...) | async-done | bytes 6291472 | tf_op jit(solution)/shard_map/psum | solution.py:697
  305.5 0.0 copy-start
  305.5 3.2 %broadcast_multiply_fusion = f32[2,1024,256]{2,1,0:T(8,128)} fusion(f32[2,1024,256]{2,1,0:T(8,128)} %get-tuple-element.72), kind=kLoop, calls=%fused_computation | loop fusion | flops 524288 | bytes 4194304 | tf_op jit(solution)/shard_map/mul | solution.py:699
  308.8 0.0 copy-done
  308.8 0.0 copy-start.1
  308.8 1.5 broadcast_multiply_fusion.1
  310.3 0.0 copy-start.2
  310.3 0.5 copy-done.1
  310.8 1.3 broadcast_multiply_fusion.2
  312.1 0.0 copy-done.2
  312.1 0.8 broadcast_multiply_fusion.3
  (1 shorter events, 0.0 us)
Async XLA Ops:
  7.2 298.4 %all-reduce.4.cloned.1.call-start = ((), (), s32[]{:S(2)}) async-start(), calls=%async_computation | async-start | bytes 12582912 | tf_op jit(solution)/shard_map/psum | solution.py:697
  144.8 0.8 copy-start.3
  144.8 0.8 copy-start.4
  144.8 0.7 copy-start.5
  144.8 0.7 copy-start.6
  144.8 0.7 copy-start.7
  144.8 0.7 copy-start.8
  144.9 0.7 copy-start.9
  144.9 0.7 copy-start.10
  144.9 0.7 copy-start.11
  305.5 3.2 %copy-start = (f32[2,256,1024]{2,1,0:T(8,128)S(1)}, f32[2,256,1024]{2,1,0:T(8,128)}, u32[]{:S(2)}) copy-start(f32[2,256,1024]{2,1,0:T(8,128)} %get-tuple-element.71) | copy-start | bytes 6291460
  308.8 2.0 copy-start.1
  310.3 1.7 copy-start.2
Sparse Core Ops, SparseCore 0:
  145.0 160.4 all-reduce.3

commit v2 on v1

--- a/solution.py
+++ b/solution.py
@@ -118,19 +118,11 @@
     fc2_b,
     out,
     input_grad,
-    g_gain1,
-    g_bias1,
+    packed,
     g_qkv,
-    g_lepe_w,
-    g_lepe_b,
     g_proj,
-    g_proj_b,
-    g_gain2,
-    g_bias2,
     g_fc1,
-    g_fc1_b,
     g_fc2,
-    g_fc2_b,
     starts,
     stage,
     x_s,
@@ -588,18 +580,169 @@
 
     @pl.when(image == images - 1)
     def _():
-        for acc, target in (
-            (acc_gain1, g_gain1),
-            (acc_bias1, g_bias1),
-            (acc_lepe_b, g_lepe_b),
-            (acc_proj_b, g_proj_b),
-            (acc_gain2, g_gain2),
-            (acc_bias2, g_bias2),
-            (acc_fc1_b, g_fc1_b),
-            (acc_fc2_b, g_fc2_b),
-        ):
-            target[...] = jnp.sum(acc[...], axis=1)
-        g_lepe_w[...] = jnp.sum(acc_lepe[...], axis=2)
+        at = 0
+        for l in range(layers):
+            for ref in big_accs:
+                rows, width = ref.shape[1:]
+                for lane in range(0, width, GROUP):
+                    packed[at : at + rows, :] = ref[l, :, lane : lane + GROUP].astype(bf16)
+                    at += rows
+        parts = []
+        for l in range(layers):
+            for acc in small_accs:
+                value = acc[l]
+                for k in range(value.size // (8 * value.shape[-1])):
+                    row = jnp.sum(value[k] if value.ndim == 3 else value, axis=0, keepdims=True)
+                    parts += [row[:, c : c + GROUP] for c in range(0, row.shape[1], GROUP)]
+        rest = packed.shape[0] - at
+        parts.append(jnp.zeros((rest - len(parts), GROUP), f32))
+        packed[at:, :] = jnp.concatenate(parts, axis=0).astype(bf16)
+
+
+def place_of(chip, core, heads):
+    return (2 * (chip // heads) + core, lax.rem(chip, heads))
+
+
+def reduce_kernel(chips, heads, mine, total, near, half, parts, own, sems):
+    core = lax.rem(lax.axis_index("dp"), 2)
+    chip = (lax.axis_index("dp") // 2) * heads + lax.axis_index("head")
+    side = 1 - core
+    rows = half.shape[0]
+    chunk = rows // chips
+    mesh_id = pl.DeviceIdType.MESH
+
+    def other(k):
+        return lax.rem(chip + k, chips)
+
+    def signal(k, carry):
+        pl.semaphore_signal(
+            barrier, inc=1, device_id=place_of(other(k), core, heads), device_id_type=mesh_id
+        )
+        return carry
+
+    barrier = pltpu.get_barrier_semaphore()
+    pl.semaphore_signal(
+        barrier, inc=1, device_id=place_of(chip, side, heads), device_id_type=mesh_id
+    )
+    lax.fori_loop(1, chips, signal, 0)
+    pl.semaphore_wait(barrier, chips)
+
+    def rows_of(ref, index, count):
+        return ref.at[pl.ds(pl.multiple_of(index * count, 16), count)]
+
+    swap = pltpu.make_async_remote_copy(
+        src_ref=rows_of(mine, side, rows),
+        dst_ref=near,
+        send_sem=sems.at[0, 0],
+        recv_sem=sems.at[1, 0],
+        device_id=place_of(chip, side, heads),
+        device_id_type=mesh_id,
+    )
+    swap.start()
+    swap.wait()
+
+    def add(k, carry):
+        at = pl.multiple_of(k * chunk, 16)
+        mine_at = pl.multiple_of(core * rows + k * chunk, 16)
+        half[pl.ds(at, chunk), :] = (
+            mine[pl.ds(mine_at, chunk), :].astype(f32) + near[pl.ds(at, chunk), :].astype(f32)
+        ).astype(bf16)
+        return carry
+
+    lax.fori_loop(0, chips, add, 0)
+
+    def scatter(k):
+        return pltpu.make_async_remote_copy(
+            src_ref=rows_of(half, other(k), chunk),
+            dst_ref=parts.at[k],
+            send_sem=sems.at[2, k],
+            recv_sem=sems.at[3, k],
+            device_id=place_of(other(k), core, heads),
+            device_id_type=mesh_id,
+        )
+
+    def start_scatter(k, carry):
+        scatter(k).start()
+        return carry
+
+    lax.fori_loop(1, chips, start_scatter, 0)
+
+    def gather(k, acc):
+        scatter(k).wait()
+        return acc + parts[k].astype(f32)
+
+    mine_sum = half[pl.ds(pl.multiple_of(chip * chunk, 16), chunk), :].astype(f32)
+    mine_sum = lax.fori_loop(1, chips, gather, mine_sum)
+    own[...] = mine_sum.astype(bf16)
+
+    def spread(k):
+        return pltpu.make_async_remote_copy(
+            src_ref=own,
+            dst_ref=rows_of(total, core * chips + chip, chunk),
+            send_sem=sems.at[4, k],
+            recv_sem=sems.at[5, k],
+            device_id=place_of(other(k), core, heads),
+            device_id_type=mesh_id,
+        )
+
+    def sent(k, source):
+        at = core * chips + lax.rem(chip + chips - k, chips)
+        return pltpu.make_async_remote_copy(
+            src_ref=source if source is not None else rows_of(total, at, chunk),
+            dst_ref=rows_of(total, at, chunk),
+            send_sem=sems.at[6, k],
+            recv_sem=sems.at[7, k],
+            device_id=place_of(chip, side, heads),
+            device_id_type=mesh_id,
+        )
+
+    def start_spread(k, carry):
+        spread(k).start()
+        return carry
+
+    lax.fori_loop(1, chips, start_spread, 0)
+    sent(0, own).start()
+    total[pl.ds(pl.multiple_of((core * chips + chip) * chunk, 16), chunk), :] = own[...]
+
+    def pass_on(k, carry):
+        spread(k).wait()
+        sent(k, None).start()
+        return carry
+
+    lax.fori_loop(1, chips, pass_on, 0)
+    sent(0, own).wait()
+
+    def finish(k, carry):
+        sent(k, None).wait()
+        return carry
+
+    lax.fori_loop(1, chips, finish, 0)
+
+
+def unpack_kernel(factor, packed, *refs):
+    g_gain1, g_bias1, g_qkv, g_lepe, g_lepe_b, g_proj, g_proj_b = refs[:7]
+    g_gain2, g_bias2, g_fc1, g_fc1_b, g_fc2, g_fc2_b = refs[7:]
+    layers = g_qkv.shape[0]
+    at = 0
+    for l in range(layers):
+        for ref in (g_qkv, g_proj, g_fc1, g_fc2):
+            rows, width = ref.shape[1:]
+            for lane in range(0, width, GROUP):
+                ref[l, :, lane : lane + GROUP] = packed[at : at + rows, :].astype(f32) * factor
+                at += rows
+    rest = packed[at:, :].astype(f32) * factor
+    row = 0
+    for l in range(layers):
+        for ref in (g_gain1, g_bias1, g_lepe, g_lepe_b, g_proj_b, g_gain2, g_bias2, g_fc1_b, g_fc2_b):
+            width = ref.shape[-1]
+            for k in range(ref.size // (layers * width)):
+                for c in range(0, width, GROUP):
+                    value = rest[row : row + 1]
+                    if ref.ndim == 3:
+                        ref[l, k : k + 1, c : c + GROUP] = value
+                    else:
+                        ref[l : l + 1, c : c + GROUP] = value
+                    row += 1
 
 
 def local(
@@ -640,17 +783,26 @@
     )
     block = pl.BlockSpec((1, tok, dim), lambda i: (i, 0, 0))
     whole = pl.BlockSpec(memory_space=pltpu.VMEM)
-    results = pl.pallas_call(
+    heads = lax.axis_size("head")
+    devices = lax.axis_size("dp") * heads
+    chips = devices // 2
+    packed_rows = sum(math.prod(w.shape) for w in weights) // GROUP
+    packed_rows = -(-packed_rows // (16 * devices)) * 16 * devices
+    out, input_grad, packed = pl.pallas_call(
         kernel,
         grid=(images,),
         out_shape=[
             jax.ShapeDtypeStruct(tokens.shape, bf16),
             jax.ShapeDtypeStruct(tokens.shape, f32),
-        ]
-        + [jax.ShapeDtypeStruct(w.shape, f32) for w in weights],
+            jax.ShapeDtypeStruct((packed_rows, GROUP), bf16),
+        ],
         in_specs=[pl.BlockSpec(memory_space=pltpu.SMEM), block, block] + [whole] * len(weights),
-        out_specs=[block, block] + [whole] * len(weights),
+        out_specs=[block, block, whole],
         scratch_shapes=[
+            pltpu.VMEM(qkv_weight.shape, f32),
+            pltpu.VMEM(proj_weight.shape, f32),
+            pltpu.VMEM(fc1_weight.shape, f32),
+            pltpu.VMEM(fc2_weight.shape, f32),
             pltpu.SMEM((BIG_CROPS + SMALL_CROPS,), jnp.int32),
             pltpu.VMEM((dim // GROUP, tok + 16, GROUP), f32),
             pltpu.VMEM((ROWS, dim), f32),
@@ -694,9 +846,33 @@
             dimension_semantics=("arbitrary",), vmem_limit_bytes=62 * 1024 * 1024
         ),
     )(crop_side, tokens, cotangent, *weights)
-    grads = lax.psum(tuple(results[2:]), ("dp", "head"))
-    factor = 1.0 / math.sqrt(lax.axis_size("dp") * lax.axis_size("head") * images * tok)
-    return (results[0], results[1]) + tuple(g * factor for g in grads)
+    half_rows = packed_rows // 2
+    chunk = half_rows // chips
+    total = pl.pallas_call(
+        partial(reduce_kernel, chips, heads),
+        out_shape=jax.ShapeDtypeStruct((packed_rows, GROUP), bf16),
+        in_specs=[whole],
+        out_specs=whole,
+        scratch_shapes=[
+            pltpu.VMEM((half_rows, GROUP), bf16),
+            pltpu.VMEM((half_rows, GROUP), bf16),
+            pltpu.VMEM((chips, chunk, GROUP), bf16),
+            pltpu.VMEM((chunk, GROUP), bf16),
+            pltpu.SemaphoreType.DMA((8, chips)),
+        ],
+        compiler_params=pltpu.CompilerParams(
+            collective_id=0, has_side_effects=True, vmem_limit_bytes=32 * 1024 * 1024
+        ),
+    )(packed)
+    factor = 1.0 / math.sqrt(devices * images * tok)
+    grads = pl.pallas_call(
+        partial(unpack_kernel, factor),
+        out_shape=[jax.ShapeDtypeStruct(w.shape, f32) for w in weights],
+        in_specs=[whole],
+        out_specs=[whole] * len(weights),
+        compiler_params=pltpu.CompilerParams(vmem_limit_bytes=32 * 1024 * 1024),
+    )(total)
+    return (out, input_grad) + tuple(grads)
 
 
 def solution(mesh):

time: 320 us -> 235 us (0.73)
  the two profiles are of different devices: /device:TPU:0 before, /device:TPU:31 now
where the time goes in v2:
time: 235 us
  Pallas kernels  231 us (98%)
  local copies, waits for them, and re-layouts  3.88 us (2%)
    pallas_call x1, Pallas kernels, local(): pl.pallas_call(kernel, grid=(images,), out_shape=[jax.ShapeDtypeStruct(to...  135 us
    pallas_call x1, Pallas kernels, local(): pl.pallas_call(partial(reduce_kernel, chips, heads), out_shape=jax.ShapeD...  92.3 us

profile of v2, /device:TPU:31, one launch (start us, length us, event | category | flops | bytes accessed | tf_op | source)
XLA Modules:
  0.0 235.1 jit_solution(13411062720980047882)
XLA Ops:
  0.6 1.3 copy.31.lepe_w
  2.0 135.0 %shard_map.271 = (bf16[4,608,256]{2,1,0:T(8,128)(2,1)}, f32[4,608,256]{2,1,0:T(8,128)}, bf16[12800,128]{1,0:T(8,128)(2,1)}) custom-call(s32[4,8]{1,0:T(4,128)} %crop_side.1, bf16[4,608,256]{2,1,0:T(8,128)(2,1)} %tokens.1, bf16[4,608,256]{2,1,0:T(8,128)(2,1)} %cotangent.1, f32[2,256]{1,0:T(2,128)} %ln1_gain.1, f32[2,256]{1,0:T(2,128)} %ln1_bias.1, ...), custom_call_target="tpu_custom_call" | custom-call | tf_op jit(solution)/shard_map/pallas_call | solution.py:791
  137.0 0.0 copy-start
  137.0 1.9 copy-done
  138.9 92.3 %shard_map.272.packed = bf16[12800,128]{1,0:T(8,128)(2,1)S(1)} custom-call(bf16[12800,128]{1,0:T(8,128)(2,1)S(1)} %copy-done), custom_call_target="tpu_custom_call" | custom-call | tf_op jit(solution)/shard_map/pallas_call | solution.py:851
  231.3 3.2 %shard_map.273 = (f32[2,256]{1,0:T(2,128)}, f32[2,256]{1,0:T(2,128)}, f32[2,256,768]{2,1,0:T(8,128)}, f32[2,9,256]{2,1,0:T(8,128)S(1)}, f32[2,256]{1,0:T(2,128)}...) custom-call(bf16[12800,128]{1,0:T(8,128)(2,1)S(1)} %shard_map.272.packed), custom_call_target="tpu_custom_call" | custom-call | tf_op jit(solution)/shard_map/pallas_call | solution.py:868
  234.5 0.6 copy.32
Async XLA Ops:
  137.0 1.9 copy-start

commit v3 on v1

--- a/solution.py
+++ b/solution.py
@@ -118,19 +118,11 @@
     fc2_b,
     out,
     input_grad,
-    g_gain1,
-    g_bias1,
+    packed,
     g_qkv,
-    g_lepe_w,
-    g_lepe_b,
     g_proj,
-    g_proj_b,
-    g_gain2,
-    g_bias2,
     g_fc1,
-    g_fc1_b,
     g_fc2,
-    g_fc2_b,
     starts,
     stage,
     x_s,
@@ -561,96 +553,400 @@
     ingest(tokens, x_s)
 
     def forward_layer(l):
-        loop(BIG_CROPS, lambda c: project(l, pl.multiple_of(c * BIG_ROWS, 16), BIG_ROWS, True))
+        for c in range(BIG_CROPS): project(l, c*BIG_ROWS, BIG_ROWS, True)
         project(l, SMALL_BASE, ROWS - SMALL_BASE, False)
-        loop(BIG_CROPS, lambda c: attend_big(l, c))
-        loop(SMALL_CROPS // 2, lambda c: attend_small(l, 2 * c, 2))
-        loop(2, lambda c: feed(l, pl.multiple_of(c * CHUNK, 16)))
-
-    loop(layers, forward_layer)
+        for c in range(BIG_CROPS): attend_big(l, c)
+        attend_small(l, 0, 6)
+        for c in range(2): feed(l, c*CHUNK)
+
+    for l in range(layers): forward_layer(l)
     emit(x_s, out)
     ingest(cotangent, e_s)
 
     def backward_layer(step):
         l = layers - 1 - step
-        loop(2, lambda c: feed_back(l, pl.multiple_of(c * CHUNK, 16)))
+        for c in range(2): feed_back(l, c*CHUNK)
         dz = e_s[...].astype(bf16)
         g_fc2[l] += mm(g_s[l], dz, TN)
         g_fc1[l] += mm(m_s[l], df_s[...], TN)
         g_proj[l] += mm(o_s[l], mid_s[...].astype(bf16), TN)
-        loop(BIG_CROPS, lambda c: attend_back_big(l, c))
-        loop(SMALL_CROPS // 2, lambda c: attend_back_small(l, 2 * c, 2))
+        for c in range(BIG_CROPS): attend_back_big(l, c)
+        attend_back_small(l, 0, 6)
         g_qkv[l] += mm(a_s[l], dqkv_s[...], TN)
-        loop(2, lambda c: project_back(l, pl.multiple_of(c * CHUNK, 16)))
-
-    loop(layers, backward_layer)
+        for c in range(2): project_back(l, c*CHUNK)
+
+    for l in range(layers): backward_layer(l)
     emit(e_s, input_grad)
 
     @pl.when(image == images - 1)
     def _():
-        for acc, target in (
-            (acc_gain1, g_gain1),
-            (acc_bias1, g_bias1),
-            (acc_lepe_b, g_lepe_b),
-            (acc_proj_b, g_proj_b),
-            (acc_gain2, g_gain2),
-            (acc_bias2, g_bias2),
-            (acc_fc1_b, g_fc1_b),
-            (acc_fc2_b, g_fc2_b),
-        ):
-            target[...] = jnp.sum(acc[...], axis=1)
-        g_lepe_w[...] = jnp.sum(acc_lepe[...], axis=2)
-
-
-def local(
-    tokens,
-    crop_side,
-    cotangent,
-    ln1_gain,
-    ln1_bias,
-    qkv_weight,
-    lepe_weight,
-    lepe_bias,
-    proj_weight,
-    proj_bias,
-    ln2_gain,
-    ln2_bias,
-    fc1_weight,
-    fc1_bias,
-    fc2_weight,
-    fc2_bias,
-):
+        at = 0
+        for l in range(layers):
+            for ref in big_accs:
+                rows, width = ref.shape[1:]
+                for lane in range(0, width, GROUP):
+                    packed[at : at + rows, :] = ref[l, :, lane : lane + GROUP].astype(bf16)
+                    at += rows
+        parts = []
+        for l in range(layers):
+            for acc in small_accs:
+                value = acc[l]
+                for k in range(value.size // (8 * value.shape[-1])):
+                    row = jnp.sum(value[k] if value.ndim == 3 else value, axis=0, keepdims=True)
+                    parts += [row[:, c : c + GROUP] for c in range(0, row.shape[1], GROUP)]
+        rest = packed.shape[0] - at
+        parts.append(jnp.zeros((rest - len(parts), GROUP), f32))
+        packed[at:, :] = jnp.concatenate(parts, axis=0).astype(bf16)
+
+
+class Grid:
+    def __init__(self, dp, heads):
+        chips = dp // 2
+        self.heads = heads
+        self.levels = next(n for n in (4, 2, 1) if chips % n == 0)
+        self.low = chips // self.levels
+        self.plane = self.low * heads
+        self.chips = chips * heads
+
+    def split(self, rows):
+        units = max(2, -(-rows // (2 * 16 * self.chips)))
+        first = max(1, (2 * units + 1) // 3)
+        return 16 * first, 16 * (units - first)
+
+    def packed_rows(self, rows):
+        return 2 * self.chips * sum(self.split(rows))
+
+    def scratch(self, rows):
+        ca, cb = self.split(rows)
+        half = self.chips * (ca + cb)
+        return [
+            pltpu.VMEM((half, GROUP), bf16),
+            pltpu.VMEM((half, GROUP), bf16),
+            pltpu.VMEM((self.plane, self.levels * ca, GROUP), bf16),
+            pltpu.VMEM((self.levels, self.plane * cb, GROUP), bf16),
+            pltpu.VMEM((1, self.levels * ca, GROUP), bf16),
+            pltpu.VMEM((1, self.plane * cb, GROUP), bf16),
+            pltpu.SemaphoreType.DMA((6, 2, self.plane)),
+            pltpu.SemaphoreType.DMA((6, 2, self.levels)),
+        ]
+
+
+def each(first, last, body):
+    def step(k, carry):
+        body(k)
+        return carry
+
+    lax.fori_loop(first, last, step, 0)
+
+
+class Here:
+    def __init__(self, grid):
+        self.grid = grid
+        dp = lax.axis_index("dp")
+        self.core = lax.rem(dp, 2)
+        chip = dp // 2
+        self.z = chip // grid.low
+        self.p = lax.rem(chip, grid.low) * grid.heads + lax.axis_index("head")
+
+    def device(self, z, p, core):
+        low = p // self.grid.heads
+        return (2 * (z * self.grid.low + low) + core, lax.rem(p, self.grid.heads))
+
+    def sibling(self):
+        return self.device(self.z, self.p, 1 - self.core)
+
+    def in_plane(self, k):
+        other = lax.rem(self.p + k, self.grid.plane)
+        return other, self.device(self.z, other, self.core)
+
+    def in_line(self, k):
+        other = lax.rem(self.z + k, self.grid.levels)
+        return other, self.device(other, self.p, self.core)
+
+    def barrier(self):
+        barrier = pltpu.get_barrier_semaphore()
+
+        def signal(device):
+            pl.semaphore_signal(
+                barrier, inc=1, device_id=device, device_id_type=pl.DeviceIdType.MESH
+            )
+
+        signal(self.sibling())
+        each(1, self.grid.plane, lambda k: signal(self.in_plane(k)[1]))
+        each(1, self.grid.levels, lambda k: signal(self.in_line(k)[1]))
+        pl.semaphore_wait(barrier, self.grid.plane + self.grid.levels - 1)
+
+
+def send(source, target, sems, device):
+    return pltpu.make_async_remote_copy(
+        src_ref=source,
+        dst_ref=target,
+        send_sem=sems[0],
+        recv_sem=sems[1],
+        device_id=device,
+        device_id_type=pl.DeviceIdType.MESH,
+    )
+
+
+class Total:
+    def __init__(self, here, mine, total, scratch):
+        self.here, self.mine, self.total = here, mine, total
+        self.near, self.half, self.a1, self.b1, self.a2, self.b2, self.sa, self.sb = scratch
+        grid = here.grid
+        self.grid = grid
+        self.ca = self.a1.shape[1] // grid.levels
+        self.cb = self.b1.shape[1] // grid.plane
+        self.rows_a = grid.chips * self.ca
+        self.rows = self.half.shape[0]
+        self.base = here.core * self.rows
+
+    def rows_at(self, ref, start, count):
+        return ref.at[pl.ds(pl.multiple_of(start, 16), count)]
+
+    def sems(self, table, stage, k):
+        return table.at[stage, 0, k], table.at[stage, 1, k]
+
+    def plane_copy(self, stage, table, source, target):
+        return lambda k: send(
+            source(k), target(k), self.sems(table, stage, k), self.here.in_plane(k)[1]
+        )
+
+    def line_copy(self, stage, table, source, target):
+        return lambda k: send(
+            source(k), target(k), self.sems(table, stage, k), self.here.in_line(k)[1]
+        )
+
+    def swap(self):
+        side = 1 - self.here.core
+        return send(
+            self.rows_at(self.mine, side * self.rows, self.rows),
+            self.near,
+            self.sems(self.sa, 0, 0),
+            self.here.sibling(),
+        )
+
+    def out_copies(self):
+        here, ca, cb = self.here, self.grid.levels * self.ca, self.grid.plane * self.cb
+        first = self.plane_copy(
+            1,
+            self.sa,
+            lambda k: self.rows_at(self.half, here.in_plane(k)[0] * ca, ca),
+            lambda k: self.a1.at[k],
+        )
+        second = self.line_copy(
+            1,
+            self.sb,
+            lambda k: self.rows_at(self.half, self.rows_a + here.in_line(k)[0] * cb, cb),
+            lambda k: self.b1.at[k],
+        )
+        return first, second
+
+    def in_copies(self):
+        here, ca, cb = self.here, self.ca, self.cb
+        first = self.line_copy(
+            2,
+            self.sb,
+            lambda k: self.rows_at(self.a1.at[0], here.in_line(k)[0] * ca, ca),
+            lambda k: self.rows_at(self.a2.at[0], k * ca, ca),
+        )
+        second = self.plane_copy(
+            2,
+            self.sa,
+            lambda k: self.rows_at(self.b1.at[0], here.in_plane(k)[0] * cb, cb),
+            lambda k: self.rows_at(self.b2.at[0], k * cb, cb),
+        )
+        return first, second
+
+    def chunk_a(self):
+        here = self.here
+        return self.base + (here.p * self.grid.levels + here.z) * self.ca
+
+    def chunk_b(self):
+        here = self.here
+        return self.base + self.rows_a + (here.z * self.grid.plane + here.p) * self.cb
+
+    def back_copies(self):
+        a = self.rows_at(self.total, self.chunk_a(), self.ca)
+        b = self.rows_at(self.total, self.chunk_b(), self.cb)
+        return (
+            self.line_copy(3, self.sb, lambda k: a, lambda k: a),
+            self.plane_copy(3, self.sa, lambda k: b, lambda k: b),
+        )
+
+    def block_a(self, p):
+        size = self.grid.levels * self.ca
+        return self.rows_at(self.total, self.base + p * size, size)
+
+    def block_b(self, z):
+        size = self.grid.plane * self.cb
+        return self.rows_at(self.total, self.base + self.rows_a + z * size, size)
+
+    def wide_copies(self):
+        a, b = self.block_a(self.here.p), self.block_b(self.here.z)
+        return (
+            self.plane_copy(4, self.sa, lambda k: a, lambda k: a),
+            self.line_copy(4, self.sb, lambda k: b, lambda k: b),
+        )
+
+    def last_copy_a(self, k):
+        grid = self.grid
+        block = self.block_a(lax.rem(self.here.p + grid.plane - k, grid.plane))
+        return send(block, block, self.sems(self.sa, 5, k), self.here.sibling())
+
+    def last_copy_b(self, k):
+        grid = self.grid
+        block = self.block_b(lax.rem(self.here.z + grid.levels - k, grid.levels))
+        return send(block, block, self.sems(self.sb, 5, k), self.here.sibling())
+
+    def start(self, copies, counts):
+        for copy, count in zip(copies, counts):
+            each(1, count, lambda k: copy(k).start())
+
+    def wait(self, copies, counts):
+        for copy, count in zip(copies, counts):
+            each(1, count, lambda k: copy(k).wait())
+
+    def step0(self):
+        self.swap().start()
+
+    def step1(self):
+        self.swap().wait()
+        size = self.ca + self.cb
+
+        def add(k):
+            at = pl.multiple_of(k * size, 16)
+            mine_at = pl.multiple_of(self.base + k * size, 16)
+            self.half[pl.ds(at, size), :] = (
+                self.mine[pl.ds(mine_at, size), :].astype(f32)
+                + self.near[pl.ds(at, size), :].astype(f32)
+            ).astype(bf16)
+
+        each(0, self.grid.chips, add)
+        self.start(self.out_copies(), (self.grid.plane, self.grid.levels))
+
+    def step2(self):
+        grid, here = self.grid, self.here
+        self.wait(self.out_copies(), (grid.plane, grid.levels))
+
+        def add(slots, own, count, chunk, chunks):
+            def body(j):
+                rows = pl.ds(pl.multiple_of(j * chunk, 16), chunk)
+                total = self.half[
+                    pl.ds(pl.multiple_of(own + j * chunk, 16), chunk), :
+                ].astype(f32)
+                total = lax.fori_loop(
+                    1, count, lambda k, acc: acc + slots[k, rows, :].astype(f32), total
+                )
+                slots[0, rows, :] = total.astype(bf16)
+
+            each(0, chunks, body)
+
+        add(self.a1, here.p * grid.levels * self.ca, grid.plane, self.ca, grid.levels)
+        add(self.b1, self.rows_a + here.z * grid.plane * self.cb, grid.levels, self.cb, grid.plane)
+        self.start(self.in_copies(), (grid.levels, grid.plane))
+
+    def step3(self):
+        grid, here = self.grid, self.here
+        self.wait(self.in_copies(), (grid.levels, grid.plane))
+
+        def add(blocks, own, slots, count, chunk, target):
+            total = blocks[0, pl.ds(pl.multiple_of(own * chunk, 16), chunk), :].astype(f32)
+            total = lax.fori_loop(
+                1,
+                count,
+                lambda k, acc: acc
+                + slots[0, pl.ds(pl.multiple_of(k * chunk, 16), chunk), :].astype(f32),
+                total,
+            )
+            self.total[pl.ds(pl.multiple_of(target, 16), chunk), :] = total.astype(bf16)
+
+        add(self.a1, here.z, self.a2, grid.levels, self.ca, self.chunk_a())
+        add(self.b1, here.p, self.b2, grid.plane, self.cb, self.chunk_b())
+        self.start(self.back_copies(), (grid.levels, grid.plane))
+
+    def step4(self):
+        grid = self.grid
+        self.wait(self.back_copies(), (grid.levels, grid.plane))
+        self.start(self.wide_copies(), (grid.plane, grid.levels))
+        self.last_copy_a(0).start()
+        self.last_copy_b(0).start()
+
+    def step5(self):
+        grid = self.grid
+        wide_a, wide_b = self.wide_copies()
+
+        def pass_a(k):
+            wide_a(k).wait()
+            self.last_copy_a(k).start()
+
+        def pass_b(k):
+            wide_b(k).wait()
+            self.last_copy_b(k).start()
+
+        each(1, grid.levels, pass_b)
+        each(1, grid.plane, pass_a)
+
+    def step6(self):
+        each(0, self.grid.plane, lambda k: self.last_copy_a(k).wait())
+        each(0, self.grid.levels, lambda k: self.last_copy_b(k).wait())
+
+
+def reduce_kernel(grid, mine, total, *scratch):
+    here = Here(grid)
+    here.barrier()
+    work = Total(here, mine, total, scratch)
+    for step in (work.step0, work.step1, work.step2, work.step3, work.step4, work.step5, work.step6):
+        step()
+
+
+def unpack_kernel(factor, packed, *refs):
+    g_gain1, g_bias1, g_qkv, g_lepe, g_lepe_b, g_proj, g_proj_b = refs[:7]
+    g_gain2, g_bias2, g_fc1, g_fc1_b, g_fc2, g_fc2_b = refs[7:]
+    layers = g_qkv.shape[0]
+    at = 0
+    for l in range(layers):
+        for ref in (g_qkv, g_proj, g_fc1, g_fc2):
+            rows, width = ref.shape[1:]
+            for lane in range(0, width, GROUP):
+                ref[l, :, lane : lane + GROUP] = packed[at : at + rows, :].astype(f32) * factor
+                at += rows
+    rest = packed[at:, :].astype(f32) * factor
+    row = 0
+    for l in range(layers):
+        for ref in (g_gain1, g_bias1, g_lepe, g_lepe_b, g_proj_b, g_gain2, g_bias2, g_fc1_b, g_fc2_b):
+            width = ref.shape[-1]
+            for k in range(ref.size // (layers * width)):
+                for c in range(0, width, GROUP):
+                    value = rest[row : row + 1]
+                    if ref.ndim == 3:
+                        ref[l, k : k + 1, c : c + GROUP] = value
+                    else:
+                        ref[l : l + 1, c : c + GROUP] = value
+                    row += 1
+
+
+def compute(packed_rows, tokens, crop_side, cotangent, *weights):
     images, tok, dim = tokens.shape
+    qkv_weight, proj_weight, fc1_weight, fc2_weight = (weights[i] for i in (2, 5, 9, 11))
     layers = qkv_weight.shape[0]
     ff = fc1_weight.shape[2]
-    weights = (
-        ln1_gain,
-        ln1_bias,
-        qkv_weight,
-        lepe_weight,
-        lepe_bias,
-        proj_weight,
-        proj_bias,
-        ln2_gain,
-        ln2_bias,
-        fc1_weight,
-        fc1_bias,
-        fc2_weight,
-        fc2_bias,
-    )
     block = pl.BlockSpec((1, tok, dim), lambda i: (i, 0, 0))
     whole = pl.BlockSpec(memory_space=pltpu.VMEM)
-    results = pl.pallas_call(
+    return pl.pallas_call(
         kernel,
         grid=(images,),
         out_shape=[
             jax.ShapeDtypeStruct(tokens.shape, bf16),
             jax.ShapeDtypeStruct(tokens.shape, f32),
-        ]
-        + [jax.ShapeDtypeStruct(w.shape, f32) for w in weights],
+            jax.ShapeDtypeStruct((packed_rows, GROUP), bf16),
+        ],
         in_specs=[pl.BlockSpec(memory_space=pltpu.SMEM), block, block] + [whole] * len(weights),
-        out_specs=[block, block] + [whole] * len(weights),
+        out_specs=[block, block, whole],
         scratch_shapes=[
+            pltpu.VMEM(qkv_weight.shape, f32),
+            pltpu.VMEM(proj_weight.shape, f32),
+            pltpu.VMEM(fc1_weight.shape, f32),
+            pltpu.VMEM(fc2_weight.shape, f32),
             pltpu.SMEM((BIG_CROPS + SMALL_CROPS,), jnp.int32),
             pltpu.VMEM((dim // GROUP, tok + 16, GROUP), f32),
             pltpu.VMEM((ROWS, dim), f32),
@@ -676,7 +972,7 @@
             pltpu.VMEM((ROWS, dim), f32),
             pltpu.VMEM((ROWS, 3 * dim), bf16),
             pltpu.VMEM((4, WIN + 48, GROUP), f32),
-            pltpu.VMEM((4, SMALL_ROWS + 32, GROUP), f32),
+            pltpu.VMEM((12, SMALL_ROWS + 32, GROUP), f32),
             pltpu.VMEM((4 * GROUP, GROUP), bf16),
             pltpu.VMEM((4 * 64, GROUP), bf16),
             pltpu.VMEM((layers, 8, ff), f32),
@@ -694,9 +990,67 @@
             dimension_semantics=("arbitrary",), vmem_limit_bytes=62 * 1024 * 1024
         ),
     )(crop_side, tokens, cotangent, *weights)
-    grads = lax.psum(tuple(results[2:]), ("dp", "head"))
-    factor = 1.0 / math.sqrt(lax.axis_size("dp") * lax.axis_size("head") * images * tok)
-    return (results[0], results[1]) + tuple(g * factor for g in grads)
+
+
+def local(
+    tokens,
+    crop_side,
+    cotangent,
+    ln1_gain,
+    ln1_bias,
+    qkv_weight,
+    lepe_weight,
+    lepe_bias,
+    proj_weight,
+    proj_bias,
+    ln2_gain,
+    ln2_bias,
+    fc1_weight,
+    fc1_bias,
+    fc2_weight,
+    fc2_bias,
+):
+    images, tok = tokens.shape[:2]
+    weights = (
+        ln1_gain,
+        ln1_bias,
+        qkv_weight,
+        lepe_weight,
+        lepe_bias,
+        proj_weight,
+        proj_bias,
+        ln2_gain,
+        ln2_bias,
+        fc1_weight,
+        fc1_bias,
+        fc2_weight,
+        fc2_bias,
+    )
+    whole = pl.BlockSpec(memory_space=pltpu.VMEM)
+    devices = lax.axis_size("dp") * lax.axis_size("head")
+    grid = Grid(lax.axis_size("dp"), lax.axis_size("head"))
+    grad_rows = sum(math.prod(w.shape) for w in weights) // GROUP
+    packed_rows = grid.packed_rows(grad_rows)
+    out, input_grad, packed = compute(packed_rows, tokens, crop_side, cotangent, *weights)
+    total = pl.pallas_call(
+        partial(reduce_kernel, grid),
+        out_shape=jax.ShapeDtypeStruct((packed_rows, GROUP), bf16),
+        in_specs=[whole],
+        out_specs=whole,
+        scratch_shapes=grid.scratch(grad_rows),
+        compiler_params=pltpu.CompilerParams(
+            collective_id=0, has_side_effects=True, vmem_limit_bytes=32 * 1024 * 1024
+        ),
+    )(packed)
+    factor = 1.0 / math.sqrt(devices * images * tok)
+    grads = pl.pallas_call(
+        partial(unpack_kernel, factor),
+        out_shape=[jax.ShapeDtypeStruct(w.shape, f32) for w in weights],
+        in_specs=[whole],
+        out_specs=[whole] * len(weights),
+        compiler_params=pltpu.CompilerParams(vmem_limit_bytes=32 * 1024 * 1024),
+    )(total)
+    return (out, input_grad) + tuple(grads)
 
 
 def solution(mesh):

time: 320 us -> 155 us (0.48)
  waiting for transfers between devices: 113 us -> 0 us
  blocking collectives: 43.8 us -> 0 us
  between operations: 14.2 us -> 0.67 us
  Pallas kernels: 136 us -> 148 us
  other arithmetic: 9.83 us -> 0 us
    psum x1 -> x0, waiting for transfers between devices: 113 us -> none  [local(): grads = lax.psum(tuple(results[2:]), ('dp', 'head'))]
    psum x1 -> x0, blocking collectives: 43.8 us -> none  [local(): grads = lax.psum(tuple(results[2:]), ('dp', 'head'))]
    pallas_call x1 -> x3, Pallas kernels: 136 us -> 148 us  [the longest x1 93.9 us: compute(): pl.pallas_call(kernel, grid=(images,), out_shape=[jax.ShapeDtypeStruct(to...]
    mul x10 -> x0, other arithmetic: 9.83 us -> none  [local(): return (results[0], results[1]) + tuple((g * factor for g in grads))]
  transfers between devices with their start and end apart: 1 -> 0, of which waited for: 1 -> 0; matrix products, arithmetic and copies ran while one was open for 1% -> 0% of each run, Pallas kernels for 0% -> 0%
where the time goes in v3:
time: 155 us; the launch traced here: 153 us
  Pallas kernels  148 us (95%)
  local copies, waits for them, and re-layouts  3.88 us (3%)
    pallas_call x1, Pallas kernels, compute(): pl.pallas_call(kernel, grid=(images,), out_shape=[jax.ShapeDtypeStruct(to...  93.9 us
    pallas_call x1, Pallas kernels, local(): pl.pallas_call(partial(reduce_kernel, grid), out_shape=jax.ShapeDtypeStru...  50.9 us
    unnamed x4, local copies, waits for them, and re-layouts  3.88 us
    pallas_call x1, Pallas kernels, local(): pl.pallas_call(partial(unpack_kernel, factor), out_shape=[jax.ShapeDtypeS...  3.24 us

profile of v3, /device:TPU:0, one launch (start us, length us, event | category | flops | bytes accessed | tf_op | source)
XLA Modules:
  0.0 152.7 jit_solution(15635964707174003075)
XLA Ops:
  0.6 1.3 copy.31.lepe_w
  2.0 93.9 %shard_map.271 = (bf16[4,608,256]{2,1,0:T(8,128)(2,1)}, f32[4,608,256]{2,1,0:T(8,128)}, bf16[12800,128]{1,0:T(8,128)(2,1)}) custom-call(s32[4,8]{1,0:T(4,128)} %crop_side.1, bf16[4,608,256]{2,1,0:T(8,128)(2,1)} %tokens.1, bf16[4,608,256]{2,1,0:T(8,128)(2,1)} %cotangent.1, f32[2,256]{1,0:T(2,128)} %ln1_gain.1, f32[2,256]{1,0:T(2,128)} %ln1_bias.1, ...), custom_call_target="tpu_custom_call" | custom-call | tf_op jit(solution)/shard_map/pallas_call | solution.py:935
  95.9 0.0 copy-start
  95.9 1.9 %copy-done = bf16[12800,128]{1,0:T(8,128)(2,1)S(1)} copy-done((bf16[12800,128]{1,0:T(8,128)(2,1)S(1)}, bf16[12800,128]{1,0:T(8,128)(2,1)}, u32[]{:S(2)}) %copy-start) | copy-done | bytes 3276824
  97.9 50.9 %shard_map.272.packed = bf16[12800,128]{1,0:T(8,128)(2,1)S(1)} custom-call(bf16[12800,128]{1,0:T(8,128)(2,1)S(1)} %copy-done), custom_call_target="tpu_custom_call" | custom-call | tf_op jit(solution)/shard_map/pallas_call | solution.py:1035
  148.8 3.2 %shard_map.273 = (f32[2,256]{1,0:T(2,128)}, f32[2,256]{1,0:T(2,128)}, f32[2,256,768]{2,1,0:T(8,128)}, f32[2,9,256]{2,1,0:T(8,128)S(1)}, f32[2,256]{1,0:T(2,128)}...) custom-call(bf16[12800,128]{1,0:T(8,128)(2,1)S(1)} %shard_map.272.packed), custom_call_target="tpu_custom_call" | custom-call | tf_op jit(solution)/shard_map/pallas_call | solution.py:1046
  152.1 0.6 copy.32
Async XLA Ops:
  95.9 1.9 %copy-start = (bf16[12800,128]{1,0:T(8,128)(2,1)S(1)}, bf16[12800,128]{1,0:T(8,128)(2,1)}, u32[]{:S(2)}) copy-start(bf16[12800,128]{1,0:T(8,128)(2,1)} %get-tuple-element.33.mine) | copy-start | bytes 9830404

commit v4 on v3

v4 whole, which is shorter than its diff:
```python
from functools import partial
import math

import jax
import jax.numpy as jnp
import numpy as np
from jax import lax
from jax.experimental import pallas as pl
from jax.experimental.pallas import tpu as pltpu
from jax.sharding import PartitionSpec as P

HEADS_GROUP = 4
HEAD_DIM = 32
SW = 7
BIG = 14
SMALL = 6
BIG_CROPS = 2
SMALL_CROPS = 6
GROUP = 128
EPSILON = 1e-05

BIG_ROWS = BIG * 16
WIN = SW * 16
SMALL_ROWS = SMALL * 8
SMALL_BASE = BIG_CROPS * BIG_ROWS
ROWS = SMALL_BASE + SMALL_CROPS * SMALL_ROWS
CHUNK = ROWS // 2

SCALE = HEAD_DIM**-0.5
LOG2E = math.log2(math.e)
NEG = -1e30

PLANE_FIRST = 0.67
VMEM_LIMIT = 63 * 1024 * 1024
FWD_SMALL = 3
BWD_SMALL = 3
LAST_STEPS = (2, 0, 2, 1, 0, 2, 1, 0, 2, 1, 0, 2, 1, 2, 0, 1, 2)

bf16 = jnp.bfloat16
f32 = jnp.float32

NN = (((1,), (0,)), ((), ()))
NT = (((1,), (1,)), ((), ()))
TN = (((0,), (0,)), ((), ()))


def mm(a, b, dims=NN):
    return lax.dot_general(a, b, dims, preferred_element_type=f32)


def iota(shape, dim):
    return lax.broadcasted_iota(jnp.int32, shape, dim)


def to_vertical(x):
    x4 = x.reshape(BIG, 2, 8, x.shape[1])
    return jnp.concatenate([x4[:, 0].reshape(WIN, -1), x4[:, 1].reshape(WIN, -1)], axis=0)


def from_vertical(y):
    y4 = y.reshape(2, BIG, 8, y.shape[1])
    return jnp.stack([y4[0], y4[1]], axis=1).reshape(BIG_ROWS, -1)


def real_big():
    sub = iota((BIG_ROWS, GROUP), 0) % 16
    return ((sub != 0) & (sub != 15)).astype(f32)


def real_small(rows):
    return ((iota((rows, GROUP), 0) % 8) < SMALL).astype(f32)


def lockstep(streams):
    streams = list(streams)
    while streams:
        left = []
        for stream in streams:
            try:
                next(stream)
                left.append(stream)
            except StopIteration:
                pass
        streams = left


def partial_rows(x):
    return jnp.sum(x.reshape(x.shape[0] // 8, 8, x.shape[1]), axis=0)


def head_mask(h):
    lane = iota((1, GROUP), 1)
    return ((lane >= h * HEAD_DIM) & (lane < (h + 1) * HEAD_DIM)).astype(f32)


def block_heads(x, keys):
    rows = x.shape[0]
    parts = []
    for h in range(HEADS_GROUP):
        part = x * head_mask(h).astype(x.dtype)
        parts.append(part)
        if keys > rows:
            parts.append(jnp.zeros((keys - rows, GROUP), x.dtype))
    return jnp.concatenate(parts, axis=0)


def ones_heads(keys):
    row_head = iota((HEADS_GROUP * keys, GROUP), 0) // keys
    lane_head = iota((HEADS_GROUP * keys, GROUP), 1) // HEAD_DIM
    return (row_head == lane_head).astype(f32).astype(bf16)


def sum_heads(x, keys, rows):
    total = None
    for h in range(HEADS_GROUP):
        part = x[h * keys : h * keys + rows] * head_mask(h)
        total = part if total is None else total + part
    return total


def keeps():
    sub = iota((8, GROUP), 0)
    return [(part).astype(f32) for part in (sub != 0, sub != 7, sub < SMALL)]


def ingest(stage, starts, source, target):
    keep_lo, keep_hi, keep_small = keeps()
    tok = source.shape[1]
    halves = source.shape[2] // GROUP
    for half in range(halves):
        stage[half, 8 : 8 + tok, :] = source[0, :, half * GROUP : (half + 1) * GROUP].astype(f32)
    for c in range(BIG_CROPS):
        yield
        start = starts[c] + 7
        for r in range(BIG):
            for half in range(halves):
                lanes = slice(half * GROUP, (half + 1) * GROUP)
                base = c * BIG_ROWS + r * 16
                lo = stage[half, pl.ds(start + r * BIG, 8), :]
                hi = stage[half, pl.ds(start + r * BIG + 8, 8), :]
                target[base : base + 8, lanes] = lo * keep_lo
                target[base + 8 : base + 16, lanes] = hi * keep_hi
    for c in range(SMALL_CROPS):
        if c % 3 == 0:
            yield
        start = starts[BIG_CROPS + c] + 8
        for r in range(SMALL):
            for half in range(halves):
                lanes = slice(half * GROUP, (half + 1) * GROUP)
                base = SMALL_BASE + c * SMALL_ROWS + r * 8
                lo = stage[half, pl.ds(start + r * SMALL, 8), :]
                target[base : base + 8, lanes] = lo * keep_small

def put(stage, half, at, value, keep):
    old = stage[half, pl.ds(at, 8), :]
    stage[half, pl.ds(at, 8), :] = jnp.where(keep > 0, value, old)

def emit(stage, starts, source, target):
    keep_lo, keep_hi, keep_small = keeps()
    tok = target.shape[1]
    halves = target.shape[2] // GROUP
    for c in range(BIG_CROPS):
        yield
        start = starts[c] + 7
        for r in range(BIG):
            for half in range(halves):
                lanes = slice(half * GROUP, (half + 1) * GROUP)
                base = c * BIG_ROWS + r * 16
                put(stage, half, start + r * BIG, source[base : base + 8, lanes].astype(f32), keep_lo)
                put(stage, half, start + r * BIG + 8, source[base + 8 : base + 16, lanes].astype(f32), keep_hi)
    for c in range(SMALL_CROPS):
        if c % 3 == 0:
            yield
        start = starts[BIG_CROPS + c] + 8
        for r in range(SMALL):
            for half in range(halves):
                lanes = slice(half * GROUP, (half + 1) * GROUP)
                base = SMALL_BASE + c * SMALL_ROWS + r * 8
                put(stage, half, start + r * SMALL, source[base : base + 8, lanes].astype(f32), keep_small)
    for half in range(halves):
        target[0, :, half * GROUP : (half + 1) * GROUP] = stage[half, 8 : 8 + tok, :].astype(
            target.dtype
        )


def place_crops(crop_side, image):
    start, n_big, n_small = jnp.int32(0), jnp.int32(0), jnp.int32(0)
    starts = [jnp.int32(0)] * (BIG_CROPS + SMALL_CROPS)
    for j in range(crop_side.shape[1]):
        side = crop_side[image, j]
        is_big = side == BIG
        slot = jnp.where(is_big, n_big, BIG_CROPS + n_small)
        for i in range(len(starts)):
            starts[i] = jnp.where(slot == i, start, starts[i])
        big_add = jnp.where(is_big, 1, 0)
        start, n_big, n_small = start + side * side, n_big + big_add, n_small + 1 - big_add
    return starts


class Env:
    def __init__(self, **refs):
        self.__dict__.update(refs)


STATE = ("n1", "r1", "a", "q", "k", "v", "eb", "es", "oat", "rdn")
STATE_FEED = ("o", "n2", "r2", "m", "g", "gp")


def state_shapes(dim, ff):
    wide = (ROWS, dim)
    shapes = dict.fromkeys(STATE + STATE_FEED, (wide, bf16))
    shapes["r1"] = shapes["r2"] = ((ROWS, GROUP), f32)
    shapes["g"] = shapes["gp"] = ((ROWS, ff), bf16)
    shapes["eb"] = ((4 * BIG_CROPS, WIN, HEADS_GROUP * GROUP), bf16)
    shapes["es"] = ((2 * SMALL_CROPS, SMALL_ROWS, HEADS_GROUP * 64), bf16)
    return shapes


GRADS = ("qkv", "proj", "fc1", "fc2")
ACCS = ("gain1", "bias1", "lepe", "lepe_b", "proj_b", "gain2", "bias2", "fc1_b", "fc2_b")


def acc_scratch(dim, ff):
    shapes = dict.fromkeys(ACCS, (8, dim))
    shapes["lepe"] = (9, 8, dim)
    shapes["fc1_b"] = (8, ff)
    return [pltpu.VMEM(shapes[name], f32) for name in ACCS]


def grad_scratch(dim, ff):
    shapes = ((dim, 3 * dim), (dim, dim), (dim, ff), (ff, dim))
    return [pltpu.VMEM(shape, f32) for shape in shapes]


def shared_scratch(dim):
    return [
        pltpu.VMEM((ROWS, dim), bf16),
        pltpu.VMEM((ROWS, 3 * dim), bf16),
        pltpu.VMEM((4 * BIG_CROPS, WIN + 48, GROUP), f32),
        pltpu.VMEM((2 * SMALL_CROPS, SMALL_ROWS + 32, GROUP), f32),
        pltpu.VMEM((4 * GROUP, GROUP), bf16),
        pltpu.VMEM((4 * 64, GROUP), bf16),
    ]


def clear(env, l):
    for ref in [getattr(env.grad[l], name) for name in GRADS] + [
        getattr(env.acc[l], name) for name in ACCS
    ]:
        ref[...] = jnp.zeros(ref.shape, f32)
    env.lepb[...] = jnp.zeros(env.lepb.shape, f32)
    env.leps[...] = jnp.zeros(env.leps.shape, f32)
    env.onesb[...] = ones_heads(GROUP)
    env.oness[...] = ones_heads(64)


def fill(packed, refs, accs):
    at = 0
    for ref in refs:
        rows, width = ref.shape
        for lane in range(0, width, GROUP):
            packed[at : at + rows, :] = ref[:, lane : lane + GROUP].astype(bf16)
            at += rows
    parts = [small_rows(acc) for acc in accs or ()]
    rest = packed.shape[0] - at - sum(part.shape[0] for part in parts)
    if rest:
        parts.append(jnp.zeros((rest, GROUP), f32))
    if parts:
        packed[at:, :] = jnp.concatenate(parts, axis=0).astype(bf16)


def small_rows(acc):
    parts = []
    for name in ACCS:
        value = getattr(acc, name)[...]
        for k in range(value.size // (8 * value.shape[-1])):
            row = jnp.sum(value[k] if value.ndim == 3 else value, axis=0, keepdims=True)
            parts += [row[:, c : c + GROUP] for c in range(0, row.shape[1], GROUP)]
    return jnp.concatenate(parts, axis=0)


def stages(env):
    dim, ff = env.dim, env.ff
    halves = dim // GROUP

    def norm_stats(x):
        center = x - jnp.mean(x, axis=1, keepdims=True)
        r = lax.rsqrt(jnp.mean(center * center, axis=1, keepdims=True) + EPSILON)
        return center * r, r

    def project(l, base, rows, big):
        rows_at = pl.ds(base, rows)
        n, r = norm_stats(env.x[rows_at, :])
        env.state[l].n1[rows_at, :] = n.astype(bf16)
        env.state[l].r1[rows_at, :] = jnp.broadcast_to(r, (rows, GROUP))
        yield
        a = (n * env.vec[l, 0:1, :dim] + env.vec[l, 1:2, :dim]).astype(bf16)
        env.state[l].a[rows_at, :] = a
        qkv = mm(a, env.qkv_w[l])
        yield
        real = real_big() if big else real_small(rows)
        for grp in range(2):
            cols = [slice(s * dim + grp * GROUP, s * dim + (grp + 1) * GROUP) for s in range(3)]
            q = qkv[:, cols[0]] * (SCALE * LOG2E)
            k = qkv[:, cols[1]]
            v = qkv[:, cols[2]] * real
            if big and grp == 1:
                q, k, v = to_vertical(q), to_vertical(k), to_vertical(v)
            lanes = slice(grp * GROUP, (grp + 1) * GROUP)
            env.state[l].q[rows_at, lanes] = q.astype(bf16)
            env.state[l].k[rows_at, lanes] = k.astype(bf16)
            env.state[l].v[rows_at, lanes] = v.astype(bf16)

    def pad_row(grp, w):
        u = iota((1, HEADS_GROUP * GROUP), 1) % GROUP
        if grp == 0:
            bad = (u % 16 == 0) | (u % 16 == 15)
        elif w == 0:
            bad = u % 8 == 0
        else:
            bad = u % 8 == 7
        return jnp.where(bad | (u >= WIN), NEG, 0.0).astype(f32)

    def pad_row_small():
        u = iota((1, HEADS_GROUP * 64), 1) % 64
        return jnp.where((u % 8 >= SMALL) | (u >= SMALL_ROWS), NEG, 0.0).astype(f32)

    def shifted(buf, idx, margin, stride, rows):
        return [buf[idx, pl.ds(margin - stride + b, rows + 2 * stride), :] for b in (-1, 0, 1)]

    def conv(views, stride, rows, weights, flip):
        total = None
        for a in range(3):
            for b in range(3):
                k = 3 * a + b
                wk = weights[8 - k : 9 - k] if flip else weights[k : k + 1]
                term = views[b][a * stride : a * stride + rows] * wk
                total = term if total is None else total + term
        return total

    def windows_big(c):
        for grp in range(2):
            for w in range(2):
                yield grp, w, c * BIG_ROWS + w * WIN

    def attend_big(l, c):
        items = list(windows_big(c))
        scores = []
        for grp, w, base in items:
            lanes = slice(grp * GROUP, (grp + 1) * GROUP)
            q = env.state[l].q[pl.ds(base, WIN), lanes]
            kb = block_heads(env.state[l].k[pl.ds(base, WIN), lanes], GROUP)
            scores.append(mm(q, kb, NT) + pad_row(grp, w))
        yield
        for i, (grp, w, base) in enumerate(items):
            parts = []
            for h in range(HEADS_GROUP):
                s = scores[i][:, h * GROUP : (h + 1) * GROUP]
                parts.append(jnp.exp2(s - jnp.max(s, axis=1, keepdims=True)).astype(bf16))
            env.state[l].eb[4 * c + 2 * grp + w] = jnp.concatenate(parts, axis=1)
        yield
        outs = []
        for i, (grp, w, base) in enumerate(items):
            lanes = slice(grp * GROUP, (grp + 1) * GROUP)
            v = env.state[l].v[pl.ds(base, WIN), lanes]
            vo = jnp.concatenate([block_heads(v, GROUP), env.onesb[...]], axis=1)
            both = mm(env.state[l].eb[4 * c + 2 * grp + w], vo)
            rden = 1.0 / both[:, GROUP:]
            oat = both[:, :GROUP] * rden
            env.state[l].rdn[pl.ds(base, WIN), lanes] = rden.astype(bf16)
            env.state[l].oat[pl.ds(base, WIN), lanes] = oat.astype(bf16)
            stride = 16 if grp == 0 else 8
            env.lepb[4 * c + i, pl.ds(24, WIN), :] = v.astype(f32)
            views = shifted(env.lepb, 4 * c + i, 24, stride, WIN)
            near = conv(views, stride, WIN, env.lepe_w[l, :, lanes], False)
            outs.append(oat + near + env.vec[l, 2:3, lanes])
            if w == 1:
                yield
        rows_at = pl.ds(c * BIG_ROWS, BIG_ROWS)
        env.state[l].o[rows_at, :GROUP] = jnp.concatenate(outs[:2], axis=0).astype(bf16)
        env.state[l].o[rows_at, GROUP:] = from_vertical(jnp.concatenate(outs[2:], axis=0)).astype(bf16)

    def attend_small(l, c0, count):
        items = [
            (grp, c0 + c, SMALL_BASE + (c0 + c) * SMALL_ROWS, 2 * (c0 + c) + grp)
            for c in range(count)
            for grp in range(2)
        ]
        low = iota((SMALL_ROWS, GROUP), 1) < 64
        scores = []
        for grp, c, base, i in items:
            lanes = slice(grp * GROUP, (grp + 1) * GROUP)
            q = env.state[l].q[pl.ds(base, SMALL_ROWS), lanes]
            kb = block_heads(env.state[l].k[pl.ds(base, SMALL_ROWS), lanes], 64)
            scores.append(mm(q, kb, NT) + pad_row_small())
        yield
        for j, (grp, c, base, i) in enumerate(items):
            parts = []
            for t in range(2):
                s = scores[j][:, t * GROUP : (t + 1) * GROUP]
                top_lo = jnp.max(jnp.where(low, s, 2 * NEG), axis=1, keepdims=True)
                top_hi = jnp.max(jnp.where(low, 2 * NEG, s), axis=1, keepdims=True)
                parts.append(jnp.exp2(s - jnp.where(low, top_lo, top_hi)).astype(bf16))
            env.state[l].es[2 * c + grp] = jnp.concatenate(parts, axis=1)
        yield
        for grp, c, base, i in items:
            lanes = slice(grp * GROUP, (grp + 1) * GROUP)
            v = env.state[l].v[pl.ds(base, SMALL_ROWS), lanes]
            vo = jnp.concatenate([block_heads(v, 64), env.oness[...]], axis=1)
            both = mm(env.state[l].es[2 * c + grp], vo)
            rden = 1.0 / both[:, GROUP:]
            oat = both[:, :GROUP] * rden
            env.state[l].rdn[pl.ds(base, SMALL_ROWS), lanes] = rden.astype(bf16)
            env.state[l].oat[pl.ds(base, SMALL_ROWS), lanes] = oat.astype(bf16)
            env.leps[i, pl.ds(16, SMALL_ROWS), :] = v.astype(f32)
            views = shifted(env.leps, i, 16, 8, SMALL_ROWS)
            near = conv(views, 8, SMALL_ROWS, env.lepe_w[l, :, lanes], False)
            env.state[l].o[pl.ds(base, SMALL_ROWS), lanes] = (oat + near + env.vec[l, 2:3, lanes]).astype(
                bf16
            )

    def feed(l, base):
        rows_at = pl.ds(base, CHUNK)
        mid = env.x[rows_at, :] + mm(env.state[l].o[rows_at, :], env.proj_w[l]) + env.vec[l, 3:4, :dim]
        yield
        n, r = norm_stats(mid)
        env.state[l].n2[rows_at, :] = n.astype(bf16)
        env.state[l].r2[rows_at, :] = jnp.broadcast_to(r, (CHUNK, GROUP))
        m = (n * env.vec[l, 4:5, :dim] + env.vec[l, 5:6, :dim]).astype(bf16)
        env.state[l].m[rows_at, :] = m
        yield
        step = 256
        for j in range(ff // step):
            cols = slice(j * step, (j + 1) * step)
            f = mm(m, env.fc1_w[l, :, cols]) + env.vec[l, 6:7, cols]
            phi = 0.5 * lax.erf(f * np.float32(math.sqrt(0.5))) + 0.5
            dens = jnp.exp2(f * f * np.float32(-0.5 * LOG2E)) * np.float32(
                1.0 / math.sqrt(2.0 * math.pi)
            )
            env.state[l].g[rows_at, cols] = (f * phi).astype(bf16)
            env.state[l].gp[rows_at, cols] = (phi + f * dens).astype(bf16)
            yield
        env.x[rows_at, :] = mid + env.vec[l, 7:8, :dim] + mm(env.state[l].g[rows_at, :], env.fc2_w[l])

    def norm_back(dm, n, r, gain):
        dn = dm * gain
        mean_one = jnp.mean(dn, axis=1, keepdims=True)
        mean_two = jnp.mean(dn * n, axis=1, keepdims=True)
        rb = jnp.concatenate([r] * halves, axis=1)
        return rb * (dn - mean_one - n * mean_two)

    def feed_back(l, base):
        rows_at = pl.ds(base, CHUNK)
        e = env.e[rows_at, :]
        dz = e.astype(bf16)
        env.dz[rows_at, :] = dz
        env.acc[l].fc2_b[...] += partial_rows(dz.astype(f32))
        yield
        step = 256
        for j in range(ff // step):
            cols = slice(j * step, (j + 1) * step)
            df = mm(dz, env.fc2_w[l, cols, :], NT) * env.state[l].gp[rows_at, cols].astype(f32)
            env.state[l].gp[rows_at, cols] = df.astype(bf16)
            env.acc[l].fc1_b[:, cols] += partial_rows(df)
            yield
        dm = mm(env.state[l].gp[rows_at, :], env.fc1_w[l], NT)
        yield
        n = env.state[l].n2[rows_at, :].astype(f32)
        env.acc[l].gain2[...] += partial_rows(dm * n)
        env.acc[l].bias2[...] += partial_rows(dm)
        dmid = e + norm_back(dm, n, env.state[l].r2[rows_at, :], env.vec[l, 4:5, :dim])
        env.mid[rows_at, :] = dmid
        yield
        dy = dmid.astype(bf16)
        env.acc[l].proj_b[...] += partial_rows(dy.astype(f32))
        env.do[rows_at, :] = mm(dy, env.proj_w[l], NT).astype(bf16).astype(f32)

    def lepe_back(l, buf, idx, margin, stride, rows, lanes, v):
        views = [buf[idx, pl.ds(margin - stride + b, rows + 2 * stride), :] for b in (-1, 0, 1)]
        vf = v.astype(f32)
        for k in range(9):
            a, b = divmod(8 - k, 3)
            env.acc[l].lepe[k, :, lanes] += partial_rows(views[b][a * stride : a * stride + rows] * vf)
        env.acc[l].lepe_b[:, lanes] += partial_rows(views[1][stride : stride + rows])
        return conv(views, stride, rows, env.lepe_w[l, :, lanes], True)

    def attend_back(l, group_items, rows, keys, buf, margin, strides, e_ref, ones, unit):
        grads = []
        kbs = []
        ds_all = []
        dop_all = []
        for grp, base, e_at, lep_at, do in group_items:
            lanes = slice(grp * GROUP, (grp + 1) * GROUP)
            rows_at = pl.ds(base, rows)
            buf[lep_at, pl.ds(margin, rows), :] = do
            dop = do * env.state[l].rdn[rows_at, lanes].astype(f32)
            tail = -(dop * env.state[l].oat[rows_at, lanes].astype(f32))
            dop_all.append(dop.astype(bf16))
            left = jnp.concatenate([dop.astype(bf16), tail.astype(bf16)], axis=1)
            vo = jnp.concatenate([block_heads(env.state[l].v[rows_at, lanes], keys), ones[...]], axis=1)
            x = mm(left, vo, NT)
            ds_all.append((e_ref[e_at].astype(f32) * x).astype(bf16))
        yield
        for i, (grp, base, e_at, lep_at, do) in enumerate(group_items):
            lanes = slice(grp * GROUP, (grp + 1) * GROUP)
            kb = block_heads(env.state[l].k[pl.ds(base, rows), lanes], keys)
            grads.append([mm(ds_all[i], kb) * SCALE])
        yield
        zero_block = jnp.zeros((rows, GROUP), bf16)
        for i in range(0, len(group_items), 2):
            pair = group_items[i : i + 2]

            def spread(first, second):
                return jnp.concatenate(
                    [
                        jnp.concatenate([first, zero_block], axis=1),
                        jnp.concatenate([zero_block, second], axis=1),
                    ],
                    axis=0,
                )

            qs = [env.state[l].q[pl.ds(it[1], rows), it[0] * GROUP : (it[0] + 1) * GROUP] for it in pair]
            dk = mm(jnp.concatenate(ds_all[i : i + 2], axis=0), spread(*qs), TN)
            es = jnp.concatenate([e_ref[it[2]] for it in pair], axis=0)
            dv = mm(es, spread(*dop_all[i : i + 2]), TN)
            for j, (grp, base, e_at, lep_at, do) in enumerate(pair):
                lanes = slice(grp * GROUP, (grp + 1) * GROUP)
                cols = slice(j * GROUP, (j + 1) * GROUP)
                near = lepe_back(
                    l, buf, lep_at, margin, strides[grp], rows, lanes, env.state[l].v[pl.ds(base, rows), lanes]
                )
                grads[i + j].append(sum_heads(dk[:, cols], keys, rows) * (1.0 / LOG2E))
                grads[i + j].append(sum_heads(dv[:, cols], keys, rows) + near)
            yield
        return grads

    def attend_back_big(l, c):
        rows_at = pl.ds(c * BIG_ROWS, BIG_ROWS)
        do_h = env.do[rows_at, :GROUP]
        do_v = to_vertical(env.do[rows_at, GROUP:])
        items = []
        for i, (grp, w, base) in enumerate(windows_big(c)):
            do = (do_h if grp == 0 else do_v)[w * WIN : (w + 1) * WIN]
            items.append((grp, base, 4 * c + 2 * grp + w, 4 * c + i, do))
        grads = yield from attend_back(l, items, WIN, GROUP, env.lepb, 24, (16, 8), env.state[l].eb, env.onesb, None)
        real = real_big()
        for s in range(3):
            left = jnp.concatenate([grads[0][s], grads[1][s]], axis=0)
            right = from_vertical(jnp.concatenate([grads[2][s], grads[3][s]], axis=0))
            if s == 2:
                left, right = left * real, right * real
            env.dqkv[rows_at, s * dim : s * dim + GROUP] = left.astype(bf16)
            env.dqkv[rows_at, s * dim + GROUP : (s + 1) * dim] = right.astype(bf16)

    def attend_back_small(l, c0, count):
        items = []
        for grp in range(2):
            for c in range(count):
                base = SMALL_BASE + (c0 + c) * SMALL_ROWS
                do = env.do[pl.ds(base, SMALL_ROWS), grp * GROUP : (grp + 1) * GROUP]
                items.append((grp, base, 2 * (c0 + c) + grp, 2 * (c0 + c) + grp, do))
        grads = yield from attend_back(l, items, SMALL_ROWS, 64, env.leps, 16, (8, 8), env.state[l].es, env.oness, None)
        real = real_small(SMALL_ROWS)
        for (grp, base, e_at, lep_at, do), grad in zip(items, grads):
            for s in range(3):
                value = grad[s] * real if s == 2 else grad[s]
                at = s * dim + grp * GROUP
                env.dqkv[pl.ds(base, SMALL_ROWS), at : at + GROUP] = value.astype(bf16)

    def project_back(l, base):
        rows_at = pl.ds(base, CHUNK)
        da = mm(env.dqkv[rows_at, :], env.qkv_w[l], NT)
        yield
        n = env.state[l].n1[rows_at, :].astype(f32)
        env.acc[l].gain1[...] += partial_rows(da * n)
        env.acc[l].bias1[...] += partial_rows(da)
        env.e_out[rows_at, :] = env.mid[rows_at, :] + norm_back(
            da, n, env.state[l].r1[rows_at, :], env.vec[l, 0:1, :dim]
        )

    def feed_grads(l):
        dz = env.dz[...]
        for j in range(0, ff, 256):
            cols = slice(j, j + 256)
            env.grad[l].fc2[cols, :] += mm(env.state[l].g[:, cols], dz, TN)
            yield
            env.grad[l].fc1[:, cols] += mm(env.state[l].m[...], env.state[l].gp[:, cols], TN)
            yield
        env.grad[l].proj[...] += mm(env.state[l].o[...], env.mid[...].astype(bf16), TN)

    def qkv_grads(l):
        for j in range(0, 3 * dim, 256):
            cols = slice(j, j + 256)
            env.grad[l].qkv[:, cols] += mm(env.state[l].a[...], env.dqkv[:, cols], TN)
            yield

    return Env(
        project=project,
        attend_big=attend_big,
        attend_small=attend_small,
        feed=feed,
        feed_back=feed_back,
        feed_grads=feed_grads,
        attend_back_big=attend_back_big,
        attend_back_small=attend_back_small,
        project_back=project_back,
        qkv_grads=qkv_grads,
    )


class Grid:
    def __init__(self, dp, heads):
        chips = dp // 2
        self.heads = heads
        self.levels = next(n for n in (4, 2, 1) if chips % n == 0)
        self.low = chips // self.levels
        self.plane = self.low * heads
        self.chips = chips * heads

    def split(self, rows):
        units = max(2, -(-rows // (2 * 16 * self.chips)))
        first = min(units - 1, max(1, round(PLANE_FIRST * units)))
        return 16 * first, 16 * (units - first)

    def packed_rows(self, rows):
        return 2 * self.chips * sum(self.split(rows))

    def scratch(self, rows):
        ca, cb = self.split(rows)
        half = self.chips * (ca + cb)
        return [
            pltpu.VMEM((half, GROUP), bf16),
            pltpu.VMEM((half, GROUP), bf16),
            pltpu.VMEM((self.plane, self.levels * ca, GROUP), bf16),
            pltpu.VMEM((self.levels, self.plane * cb, GROUP), bf16),
            pltpu.VMEM((1, self.levels * ca, GROUP), bf16),
            pltpu.VMEM((1, self.plane * cb, GROUP), bf16),
            pltpu.SemaphoreType.DMA((6, 2, self.plane)),
            pltpu.SemaphoreType.DMA((6, 2, self.levels)),
            pltpu.SemaphoreType.REGULAR,
        ]


def each(first, last, body):
    def step(k, carry):
        body(k)
        return carry

    lax.fori_loop(first, last, step, 0)


class Here:
    def __init__(self, grid):
        self.grid = grid
        dp = lax.axis_index("dp")
        self.core = lax.rem(dp, 2)
        chip = dp // 2
        self.z = chip // grid.low
        self.p = lax.rem(chip, grid.low) * grid.heads + lax.axis_index("head")

    def device(self, z, p, core):
        low = p // self.grid.heads
        return (2 * (z * self.grid.low + low) + core, lax.rem(p, self.grid.heads))

    def sibling(self):
        return self.device(self.z, self.p, 1 - self.core)

    def in_plane(self, k):
        other = lax.rem(self.p + k, self.grid.plane)
        return other, self.device(self.z, other, self.core)

    def in_line(self, k):
        other = lax.rem(self.z + k, self.grid.levels)
        return other, self.device(other, self.p, self.core)

    def greet(self):
        barrier = pltpu.get_barrier_semaphore()

        def signal(device):
            pl.semaphore_signal(
                barrier, inc=1, device_id=device, device_id_type=pl.DeviceIdType.MESH
            )

        signal(self.sibling())
        each(1, self.grid.plane, lambda k: signal(self.in_plane(k)[1]))
        each(1, self.grid.levels, lambda k: signal(self.in_line(k)[1]))

    def wait(self):
        pl.semaphore_wait(
            pltpu.get_barrier_semaphore(), self.grid.plane + self.grid.levels - 1
        )


def send(source, target, sems, device):
    return pltpu.make_async_remote_copy(
        src_ref=source,
        dst_ref=target,
        send_sem=sems[0],
        recv_sem=sems[1],
        device_id=device,
        device_id_type=pl.DeviceIdType.MESH,
    )


class Total:
    def __init__(self, here, mine, total, scratch):
        self.here, self.mine, self.total = here, mine, total
        self.near, self.half, self.a1, self.b1, self.a2, self.b2 = scratch[:6]
        self.sa, self.sb, self.free = scratch[6:]
        grid = here.grid
        self.grid = grid
        self.ca = self.a1.shape[1] // grid.levels
        self.cb = self.b1.shape[1] // grid.plane
        self.rows_a = grid.chips * self.ca
        self.rows = self.half.shape[0]
        self.base = here.core * self.rows

    def rows_at(self, ref, start, count):
        return ref.at[pl.ds(pl.multiple_of(start, 16), count)]

    def sems(self, table, stage, k):
        return table.at[stage, 0, k], table.at[stage, 1, k]

    def plane_copy(self, stage, table, source, target):
        return lambda k: send(
            source(k), target(k), self.sems(table, stage, k), self.here.in_plane(k)[1]
        )

    def line_copy(self, stage, table, source, target):
        return lambda k: send(
            source(k), target(k), self.sems(table, stage, k), self.here.in_line(k)[1]
        )

    def swap(self):
        side = 1 - self.here.core
        return send(
            self.rows_at(self.mine, side * self.rows, self.rows),
            self.near,
            self.sems(self.sa, 0, 0),
            self.here.sibling(),
        )

    def out_copies(self):
        here, ca, cb = self.here, self.grid.levels * self.ca, self.grid.plane * self.cb
        first = self.plane_copy(
            1,
            self.sa,
            lambda k: self.rows_at(self.half, here.in_plane(k)[0] * ca, ca),
            lambda k: self.a1.at[k],
        )
        second = self.line_copy(
            1,
            self.sb,
            lambda k: self.rows_at(self.half, self.rows_a + here.in_line(k)[0] * cb, cb),
            lambda k: self.b1.at[k],
        )
        return first, second

    def in_copies(self):
        here, ca, cb = self.here, self.ca, self.cb
        first = self.line_copy(
            2,
            self.sb,
            lambda k: self.rows_at(self.a1.at[0], here.in_line(k)[0] * ca, ca),
            lambda k: self.rows_at(self.a2.at[0], k * ca, ca),
        )
        second = self.plane_copy(
            2,
            self.sa,
            lambda k: self.rows_at(self.b1.at[0], here.in_plane(k)[0] * cb, cb),
            lambda k: self.rows_at(self.b2.at[0], k * cb, cb),
        )
        return first, second

    def chunk_a(self):
        here = self.here
        return self.base + (here.p * self.grid.levels + here.z) * self.ca

    def chunk_b(self):
        here = self.here
        return self.base + self.rows_a + (here.z * self.grid.plane + here.p) * self.cb

    def back_copies(self):
        a = self.rows_at(self.total, self.chunk_a(), self.ca)
        b = self.rows_at(self.total, self.chunk_b(), self.cb)
        return (
            self.line_copy(3, self.sb, lambda k: a, lambda k: a),
            self.plane_copy(3, self.sa, lambda k: b, lambda k: b),
        )

    def block_a(self, p):
        size = self.grid.levels * self.ca
        return self.rows_at(self.total, self.base + p * size, size)

    def block_b(self, z):
        size = self.grid.plane * self.cb
        return self.rows_at(self.total, self.base + self.rows_a + z * size, size)

    def wide_copies(self):
        a, b = self.block_a(self.here.p), self.block_b(self.here.z)
        return (
            self.plane_copy(4, self.sa, lambda k: a, lambda k: a),
            self.line_copy(4, self.sb, lambda k: b, lambda k: b),
        )

    def last_copy_a(self, k):
        grid = self.grid
        block = self.block_a(lax.rem(self.here.p + grid.plane - k, grid.plane))
        return send(block, block, self.sems(self.sa, 5, k), self.here.sibling())

    def last_copy_b(self, k):
        grid = self.grid
        block = self.block_b(lax.rem(self.here.z + grid.levels - k, grid.levels))
        return send(block, block, self.sems(self.sb, 5, k), self.here.sibling())

    def start(self, copies, counts):
        for copy, count in zip(copies, counts):
            each(1, count, lambda k: copy(k).start())

    def wait(self, copies, counts):
        for copy, count in zip(copies, counts):
            each(1, count, lambda k: copy(k).wait())

    def steps(self):
        return (
            self.step0,
            self.step1,
            self.step2,
            self.step3,
            self.step4,
            self.step5,
            self.step6,
        )

    def step0(self):
        self.swap().start()

    def step1(self):
        self.swap().wait()
        pl.semaphore_signal(
            self.free,
            inc=1,
            device_id=self.here.sibling(),
            device_id_type=pl.DeviceIdType.MESH,
        )
        size = self.ca + self.cb

        def add(k):
            at = pl.multiple_of(k * size, 16)
            mine_at = pl.multiple_of(self.base + k * size, 16)
            self.half[pl.ds(at, size), :] = (
                self.mine[pl.ds(mine_at, size), :].astype(f32)
                + self.near[pl.ds(at, size), :].astype(f32)
            ).astype(bf16)

        each(0, self.grid.chips, add)
        self.start(self.out_copies(), (self.grid.plane, self.grid.levels))

    def step2(self):
        grid, here = self.grid, self.here
        self.wait(self.out_copies(), (grid.plane, grid.levels))

        def add(slots, own, count, chunk, chunks):
            def body(j):
                rows = pl.ds(pl.multiple_of(j * chunk, 16), chunk)
                total = self.half[
                    pl.ds(pl.multiple_of(own + j * chunk, 16), chunk), :
                ].astype(f32)
                total = lax.fori_loop(
                    1, count, lambda k, acc: acc + slots[k, rows, :].astype(f32), total
                )
                slots[0, rows, :] = total.astype(bf16)

            each(0, chunks, body)

        add(self.a1, here.p * grid.levels * self.ca, grid.plane, self.ca, grid.levels)
        add(self.b1, self.rows_a + here.z * grid.plane * self.cb, grid.levels, self.cb, grid.plane)
        self.start(self.in_copies(), (grid.levels, grid.plane))

    def step3(self):
        grid, here = self.grid, self.here
        self.wait(self.in_copies(), (grid.levels, grid.plane))

        def add(blocks, own, slots, count, chunk, target):
            total = blocks[0, pl.ds(pl.multiple_of(own * chunk, 16), chunk), :].astype(f32)
            total = lax.fori_loop(
                1,
                count,
                lambda k, acc: acc
                + slots[0, pl.ds(pl.multiple_of(k * chunk, 16), chunk), :].astype(f32),
                total,
            )
            self.total[pl.ds(pl.multiple_of(target, 16), chunk), :] = total.astype(bf16)

        add(self.a1, here.z, self.a2, grid.levels, self.ca, self.chunk_a())
        add(self.b1, here.p, self.b2, grid.plane, self.cb, self.chunk_b())
        self.start(self.back_copies(), (grid.levels, grid.plane))

    def step4(self):
        grid = self.grid
        self.wait(self.back_copies(), (grid.levels, grid.plane))
        self.start(self.wide_copies(), (grid.plane, grid.levels))
        pl.semaphore_wait(self.free, 1)
        self.last_copy_a(0).start()
        self.last_copy_b(0).start()

    def step5(self):
        grid = self.grid
        wide_a, wide_b = self.wide_copies()

        def pass_a(k):
            wide_a(k).wait()
            self.last_copy_a(k).start()

        def pass_b(k):
            wide_b(k).wait()
            self.last_copy_b(k).start()

        each(1, grid.levels, pass_b)
        each(1, grid.plane, pass_a)

    def step6(self):
        each(0, self.grid.plane, lambda k: self.last_copy_a(k).wait())
        each(0, self.grid.levels, lambda k: self.last_copy_b(k).wait())


def main_kernel(
    grid,
    crop_side,
    tokens,
    cotangent,
    ln1_gain,
    ln1_bias,
    qkv_w,
    lepe_w,
    lepe_b,
    proj_w,
    proj_b,
    ln2_gain,
    ln2_bias,
    fc1_w,
    fc1_b,
    fc2_w,
    fc2_b,
    out,
    e_out,
    *refs,
):
    names = STATE + STATE_FEED
    totals, packed, sem_out, refs = refs[:3], refs[3:6], refs[6], refs[7:]
    layers = qkv_w.shape[0]
    state, grad, acc = {}, {}, {}
    for l in range(layers):
        state[l], refs = Env(**dict(zip(names, refs))), refs[len(names) :]
        grad[l], refs = Env(**dict(zip(GRADS, refs))), refs[len(GRADS) :]
        acc[l], refs = Env(**dict(zip(ACCS, refs))), refs[len(ACCS) :]
    dz, dqkv, lepb, leps, onesb, oness, stage, x, mid, do, vec = refs[:11]
    refs = refs[11:]
    e = x
    count = len(refs) // 3
    here = Here(grid)
    sums = [
        Total(here, ref, ref, refs[i * count : (i + 1) * count]) for i, ref in enumerate(packed)
    ]
    image = pl.program_id(0)
    env = Env(
        dim=tokens.shape[2],
        ff=fc1_w.shape[2],
        state=state,
        grad=grad,
        acc=acc,
        dz=dz,
        dqkv=dqkv,
        lepb=lepb,
        leps=leps,
        onesb=onesb,
        oness=oness,
        x=x,
        mid=mid,
        e=e,
        do=do,
        vec=vec,
        e_out=e,
        qkv_w=qkv_w,
        proj_w=proj_w,
        fc1_w=fc1_w,
        fc2_w=fc2_w,
        lepe_w=lepe_w,
    )

    @pl.when(image == 0)
    def _():
        here.greet()
        for l in range(layers):
            clear(env, l)
            for i, ref in enumerate(
                (ln1_gain, ln1_bias, lepe_b, proj_b, ln2_gain, ln2_bias, fc1_b, fc2_b)
            ):
                vec[l, i : i + 1, : ref.shape[1]] = ref[l : l + 1, :]
        stage[...] = jnp.zeros(stage.shape, f32)

    def last_image(body):
        pl.when(image == pl.num_programs(0) - 1)(body)

    starts = place_crops(crop_side, image)
    run = stages(env)
    lockstep([ingest(stage, starts, tokens, x)])
    for l in range(layers):
        units = [run.project(l, c * BIG_ROWS, BIG_ROWS, True) for c in range(BIG_CROPS)]
        units.append(run.project(l, SMALL_BASE, ROWS - SMALL_BASE, False))
        lockstep(units)
        lockstep(
            [run.attend_big(l, c) for c in range(BIG_CROPS)]
            + [run.attend_small(l, c, FWD_SMALL) for c in range(0, SMALL_CROPS, FWD_SMALL)]
        )
        lockstep(run.feed(l, c * CHUNK) for c in range(2))
    out[0] = x[...].astype(bf16)
    lockstep([ingest(stage, starts, cotangent, e)])

    def attend_back(l):
        return [run.attend_back_big(l, c) for c in range(BIG_CROPS)] + [
            run.attend_back_small(l, c, BWD_SMALL) for c in range(0, SMALL_CROPS, BWD_SMALL)
        ]

    def project_back(l):
        return [run.project_back(l, c * CHUNK) for c in range(2)]

    for l in reversed(range(1, layers)):
        lockstep([run.feed_back(l, c * CHUNK) for c in range(2)])
        lockstep(attend_back(l) + [run.feed_grads(l)])
        lockstep(project_back(l) + [run.qkv_grads(l)])

    @last_image
    def _():
        refs = [getattr(grad[l], name) for l in range(1, layers) for name in GRADS]
        fill(packed[0], refs, None)
        here.wait()
        sums[0].step0()

    lockstep([run.feed_back(0, c * CHUNK) for c in range(2)])

    @last_image
    def _():
        sums[0].step1()

    lockstep([run.feed_grads(0)])

    @last_image
    def _():
        fill(packed[1], [grad[0].fc1, grad[0].fc2, grad[0].proj], None)
        sums[1].step0()

    lockstep(attend_back(0))

    @last_image
    def _():
        sums[1].step1()

    lockstep(project_back(0) + [run.qkv_grads(0)])
    e_out[0] = e[...]

    @last_image
    def _():
        fill(packed[2], [grad[0].qkv], [acc[l] for l in range(layers)])
        done = [2, 2, 0]
        for which in LAST_STEPS:
            sums[which].steps()[done[which]]()
            done[which] += 1
            if done[which] == 7:
                pltpu.make_async_copy(packed[which], totals[which], sem_out.at[which]).start()
        for which in range(3):
            pltpu.make_async_copy(packed[which], totals[which], sem_out.at[which]).wait()


def last_kernel(factor, crop_side, x, e, total1, total2, total3, out, input_grad, *refs):
    g_gain1, g_bias1, g_qkv, g_lepe, g_lepe_b, g_proj, g_proj_b = refs[:7]
    g_gain2, g_bias2, g_fc1, g_fc1_b, g_fc2, g_fc2_b = refs[7:13]
    stage, held1, held2, held3, w_qkv, w_proj, w_fc1, w_fc2, sem_in, sem_out = refs[13:]
    layers = g_qkv.shape[0]
    image = pl.program_id(0)
    loads = [
        pltpu.make_async_copy(total, held, sem_in.at[i])
        for i, (total, held) in enumerate(
            ((total1, held1), (total2, held2), (total3, held3))
        )
    ]
    big = ((w_qkv, g_qkv), (w_proj, g_proj), (w_fc1, g_fc1), (w_fc2, g_fc2))
    stores = [
        [
            pltpu.make_async_copy(made.at[l], target.at[l], sem_out.at[i, l])
            for i, (made, target) in enumerate(big)
        ]
        for l in range(layers)
    ]

    def unpack(packed, l, which):
        at = 0
        for i in which:
            ref = big[i][0]
            rows, width = ref.shape[1:]
            for lane in range(0, width, GROUP):
                ref[l, :, lane : lane + GROUP] = packed[at : at + rows, :].astype(f32) * factor
                at += rows
            stores[l][i].start()
        return at

    @pl.when(image == 0)
    def _():
        for load in loads:
            load.start()

    starts = place_crops(crop_side, image)
    lockstep(
        [emit(stage.at[0], starts, x.at[0], out), emit(stage.at[1], starts, e.at[0], input_grad)]
    )

    @pl.when(image == 0)
    def _():
        loads[0].wait()
        at = 0
        for l in range(1, layers):
            at += unpack(held1.at[at:] if at else held1, l, range(4))
        loads[1].wait()
        unpack(held2, 0, (2, 3, 1))
        loads[2].wait()
        at = unpack(held3, 0, (0,))
        rest = held3[at:, :].astype(f32) * factor
        row = 0
        for l in range(layers):
            for ref in (
                g_gain1,
                g_bias1,
                g_lepe,
                g_lepe_b,
                g_proj_b,
                g_gain2,
                g_bias2,
                g_fc1_b,
                g_fc2_b,
            ):
                width = ref.shape[-1]
                for k in range(ref.size // (layers * width)):
                    for c in range(0, width, GROUP):
                        value = rest[row : row + 1]
                        if ref.ndim == 3:
                            ref[l, k : k + 1, c : c + GROUP] = value
                        else:
                            ref[l : l + 1, c : c + GROUP] = value
                        row += 1

    @pl.when(image == pl.num_programs(0) - 1)
    def _():
        for layer in stores:
            for store in layer:
                store.wait()


def local(tokens, crop_side, cotangent, *weights):
    images, tok, dim = tokens.shape
    qkv_w, proj_w, fc1_w, fc2_w = (weights[i] for i in (2, 5, 9, 11))
    layers = qkv_w.shape[0]
    ff = fc1_w.shape[2]
    devices = lax.axis_size("dp") * lax.axis_size("head")
    grid = Grid(lax.axis_size("dp"), lax.axis_size("head"))
    grad_rows = [w.size // (layers * GROUP) for w in (qkv_w, proj_w, fc1_w, fc2_w)]
    small_rows_all = sum(w.size for w in weights) // GROUP - layers * sum(grad_rows)
    parts = [
        (layers - 1) * sum(grad_rows),
        sum(grad_rows[1:]),
        grad_rows[0] + small_rows_all,
    ]
    packed_rows = [grid.packed_rows(rows) for rows in parts]

    whole = pl.BlockSpec(memory_space=pltpu.VMEM)
    smem = pl.BlockSpec(memory_space=pltpu.SMEM)
    anywhere = pl.BlockSpec(memory_space=pl.ANY)
    block = pl.BlockSpec((1, tok, dim), lambda i: (i, 0, 0))
    canonical = pl.BlockSpec((1, ROWS, dim), lambda i: (i, 0, 0))
    shapes = state_shapes(dim, ff)
    packed_types = [jax.ShapeDtypeStruct((rows, GROUP), bf16) for rows in packed_rows]
    out, e, *totals = pl.pallas_call(
        partial(main_kernel, grid),
        grid=(images,),
        out_shape=[
            jax.ShapeDtypeStruct((images, ROWS, dim), bf16),
            jax.ShapeDtypeStruct((images, ROWS, dim), f32),
        ]
        + packed_types,
        in_specs=[smem, block, block] + [whole] * len(weights),
        out_specs=[canonical, canonical] + [anywhere] * len(packed_rows),
        scratch_shapes=[pltpu.VMEM(part.shape, bf16) for part in packed_types]
        + [pltpu.SemaphoreType.DMA((3,))]
        + layers
        * (
            [pltpu.VMEM(*shapes[name]) for name in STATE + STATE_FEED]
            + grad_scratch(dim, ff)
            + acc_scratch(dim, ff)
        )
        + shared_scratch(dim)
        + [
            pltpu.VMEM((dim // GROUP, tok + 16, GROUP), f32),
            pltpu.VMEM((ROWS, dim), f32),
            pltpu.VMEM((ROWS, dim), f32),
            pltpu.VMEM((ROWS, dim), f32),
            pltpu.VMEM((layers, 8, ff), f32),
        ]
        + [scratch for rows in parts for scratch in grid.scratch(rows)],
        compiler_params=pltpu.CompilerParams(
            dimension_semantics=("arbitrary",),
            collective_id=0,
            has_side_effects=True,
            vmem_limit_bytes=VMEM_LIMIT,
        ),
    )(crop_side, tokens, cotangent, *weights)

    factor = 1.0 / math.sqrt(devices * images * tok)
    big = (2, 5, 9, 11)
    return pl.pallas_call(
        partial(last_kernel, factor),
        grid=(images,),
        out_shape=[
            jax.ShapeDtypeStruct(tokens.shape, bf16),
            jax.ShapeDtypeStruct(tokens.shape, f32),
        ]
        + [jax.ShapeDtypeStruct(w.shape, f32) for w in weights],
        in_specs=[smem, canonical, canonical] + [anywhere] * len(totals),
        out_specs=[block, block]
        + [anywhere if i in big else whole for i in range(len(weights))],
        scratch_shapes=[pltpu.VMEM((2, dim // GROUP, tok + 16, GROUP), f32)]
        + [pltpu.VMEM(part.shape, bf16) for part in packed_types]
        + [pltpu.VMEM(weights[i].shape, f32) for i in big]
        + [pltpu.SemaphoreType.DMA((3,)), pltpu.SemaphoreType.DMA((4, layers))],
        compiler_params=pltpu.CompilerParams(
            dimension_semantics=("arbitrary",), vmem_limit_bytes=VMEM_LIMIT
        ),
    )(crop_side, out, e, *totals)


def solution(mesh):
    sharded = P(("dp", "head"), None, None)
    return jax.shard_map(
        local,
        mesh=mesh,
        in_specs=(sharded, P(("dp", "head"), None), sharded) + (P(),) * 13,
        out_specs=(sharded, sharded) + (P(),) * 13,
        check_vma=False,
    )
```

time: 155 us -> 147 us (0.948); the launches traced: 153 us -> 147 us
  Pallas kernels: 148 us -> 143 us
    pallas_call x3 -> x2, Pallas kernels: 148 us -> 143 us  [the longest x1 134 us: local(): pl.pallas_call(partial(main_kernel, grid), grid=(images,), out_shape=[jax...]
    unnamed x4 -> x1, local copies, waits for them, and re-layouts: 3.88 us -> 1.34 us
where the time goes in v4:
time: 147 us
  Pallas kernels  143 us (97%)
  local copies, waits for them, and re-layouts  2.72 us (2%)
    pallas_call x1, Pallas kernels, local(): pl.pallas_call(partial(main_kernel, grid), grid=(images,), out_shape=[jax...  134 us
    pallas_call x1, Pallas kernels, local(): pl.pallas_call(partial(last_kernel, factor), grid=(images,), out_shape=[j...  8.84 us

profile of v4, /device:TPU:0, one launch (start us, length us, event | category | flops | bytes accessed | tf_op | source)
XLA Modules:
  0.0 146.7 jit_solution(7944314780278998224)
XLA Ops:
  0.6 1.3 copy.31.lepe_w
  2.0 134.5 %shard_map.271 = (bf16[4,736,256]{2,1,0:T(8,128)(2,1)}, f32[4,736,256]{2,1,0:T(8,128)}, bf16[6144,128]{1,0:T(8,128)(2,1)}, bf16[4608,128]{1,0:T(8,128)(2,1)}, bf16[2048,128]{1,0:T(8,128)(2,1)}) custom-call(s32[4,8]{1,0:T(4,128)} %crop_side.3, bf16[4,608,256]{2,1,0:T(8,128)(2,1)} %tokens.1, bf16[4,608,256]{2,1,0:T(8,128)(2,1)} %cotangent.1, ...), custom_call_target="tpu_custom_call" | custom-call | tf_op jit(solution)/shard_map/pallas_call | solution.py:1181
  136.5 8.8 %shard_map.272 = (bf16[4,608,256]{2,1,0:T(8,128)(2,1)}, f32[4,608,256]{2,1,0:T(8,128)}, f32[2,256]{1,0:T(2,128)}, f32[2,256]{1,0:T(2,128)}, f32[2,256,768]{2,1,0...) custom-call(s32[4,8]{1,0:T(4,128)} %crop_side.3, ...), custom_call_target="tpu_custom_call" | custom-call | tf_op jit(solution)/shard_map/pallas_call | solution.py:1218
  145.3 1.4 copy.32

commit v5 on v4

--- a/solution.py
+++ b/solution.py
@@ -29,12 +29,13 @@
 SCALE = HEAD_DIM**-0.5
 LOG2E = math.log2(math.e)
 NEG = -1e30
+ROOT_HALF = math.sqrt(0.5)
 
 PLANE_FIRST = 0.67
 VMEM_LIMIT = 63 * 1024 * 1024
 FWD_SMALL = 3
 BWD_SMALL = 3
-LAST_STEPS = (2, 0, 2, 1, 0, 2, 1, 0, 2, 1, 0, 2, 1, 2, 0, 1, 2)
+LAST_STEPS = (2, 2, 0, 1, 2, 0, 1, 2, 0, 1, 2, 0, 1, 2, 0, 1, 2)
 
 bf16 = jnp.bfloat16
 f32 = jnp.float32
@@ -111,10 +112,10 @@
 
 
 def sum_heads(x, keys, rows):
-    total = None
-    for h in range(HEADS_GROUP):
-        part = x[h * keys : h * keys + rows] * head_mask(h)
-        total = part if total is None else total + part
+    lane = iota((1, GROUP), 1)
+    total = x[:rows]
+    for h in range(1, HEADS_GROUP):
+        total = jnp.where(lane >= h * HEAD_DIM, x[h * keys : h * keys + rows], total)
     return total
 
 
@@ -426,21 +427,23 @@
         n, r = norm_stats(mid)
         env.state[l].n2[rows_at, :] = n.astype(bf16)
         env.state[l].r2[rows_at, :] = jnp.broadcast_to(r, (CHUNK, GROUP))
-        m = (n * env.vec[l, 4:5, :dim] + env.vec[l, 5:6, :dim]).astype(bf16)
+        m = (n * env.vec[l, 8:9, :dim] + env.vec[l, 5:6, :dim]).astype(bf16)
         env.state[l].m[rows_at, :] = m
         yield
         step = 256
         for j in range(ff // step):
             cols = slice(j * step, (j + 1) * step)
             f = mm(m, env.fc1_w[l, :, cols]) + env.vec[l, 6:7, cols]
-            phi = 0.5 * lax.erf(f * np.float32(math.sqrt(0.5))) + 0.5
-            dens = jnp.exp2(f * f * np.float32(-0.5 * LOG2E)) * np.float32(
-                1.0 / math.sqrt(2.0 * math.pi)
-            )
-            env.state[l].g[rows_at, cols] = (f * phi).astype(bf16)
-            env.state[l].gp[rows_at, cols] = (phi + f * dens).astype(bf16)
+            twice = lax.erf(f) + 1.0
+            dens = jnp.exp2(f * f * np.float32(-LOG2E)) * np.float32(2.0 / math.sqrt(math.pi))
+            env.state[l].g[rows_at, cols] = (f * twice).astype(bf16)
+            env.state[l].gp[rows_at, cols] = (twice + f * dens).astype(bf16)
             yield
-        env.x[rows_at, :] = mid + env.vec[l, 7:8, :dim] + mm(env.state[l].g[rows_at, :], env.fc2_w[l])
+        env.x[rows_at, :] = (
+            mid
+            + env.vec[l, 7:8, :dim]
+            + mm(env.state[l].g[rows_at, :], env.fc2_w[l]) * np.float32(ROOT_HALF)
+        )
 
     def norm_back(dm, n, r, gain):
         dn = dm * gain
@@ -454,12 +457,13 @@
         e = env.e[rows_at, :]
         dz = e.astype(bf16)
         env.dz[rows_at, :] = dz
+        half_dz = (0.5 * e).astype(bf16)
         env.acc[l].fc2_b[...] += partial_rows(dz.astype(f32))
         yield
         step = 256
         for j in range(ff // step):
             cols = slice(j * step, (j + 1) * step)
-            df = mm(dz, env.fc2_w[l, cols, :], NT) * env.state[l].gp[rows_at, cols].astype(f32)
+            df = mm(half_dz, env.fc2_w[l, cols, :], NT) * env.state[l].gp[rows_at, cols].astype(f32)
             env.state[l].gp[rows_at, cols] = df.astype(bf16)
             env.acc[l].fc1_b[:, cols] += partial_rows(df)
             yield
@@ -641,12 +645,29 @@
         ]
 
 
+def aligned(start):
+    return start if isinstance(start, int) else pl.multiple_of(start, 16)
+
+
 def each(first, last, body):
+    if last - first <= 4:
+        for k in range(first, last):
+            body(k)
+        return
+
     def step(k, carry):
         body(k)
         return carry
 
     lax.fori_loop(first, last, step, 0)
+
+
+def add_up(first, last, total, term):
+    if last - first <= 4:
+        for k in range(first, last):
+            total = total + term(k)
+        return total
+    return lax.fori_loop(first, last, lambda k, acc: acc + term(k), total)
 
 
 class Here:
@@ -716,7 +737,7 @@
         self.base = here.core * self.rows
 
     def rows_at(self, ref, start, count):
-        return ref.at[pl.ds(pl.multiple_of(start, 16), count)]
+        return ref.at[pl.ds(aligned(start), count)]
 
     def sems(self, table, stage, k):
         return table.at[stage, 0, k], table.at[stage, 1, k]
@@ -843,17 +864,18 @@
             device_id=self.here.sibling(),
             device_id_type=pl.DeviceIdType.MESH,
         )
-        size = self.ca + self.cb
+        slabs = 4 if self.grid.chips % 4 == 0 else 1
+        size = (self.ca + self.cb) * self.grid.chips // slabs
 
         def add(k):
-            at = pl.multiple_of(k * size, 16)
+            at = aligned(k * size)
             mine_at = pl.multiple_of(self.base + k * size, 16)
             self.half[pl.ds(at, size), :] = (
                 self.mine[pl.ds(mine_at, size), :].astype(f32)
                 + self.near[pl.ds(at, size), :].astype(f32)
             ).astype(bf16)
 
-        each(0, self.grid.chips, add)
+        each(0, slabs, add)
         self.start(self.out_copies(), (self.grid.plane, self.grid.levels))
 
     def step2(self):
@@ -862,13 +884,11 @@
 
         def add(slots, own, count, chunk, chunks):
             def body(j):
-                rows = pl.ds(pl.multiple_of(j * chunk, 16), chunk)
+                rows = pl.ds(aligned(j * chunk), chunk)
                 total = self.half[
                     pl.ds(pl.multiple_of(own + j * chunk, 16), chunk), :
                 ].astype(f32)
-                total = lax.fori_loop(
-                    1, count, lambda k, acc: acc + slots[k, rows, :].astype(f32), total
-                )
+                total = add_up(1, count, total, lambda k: slots[k, rows, :].astype(f32))
                 slots[0, rows, :] = total.astype(bf16)
 
             each(0, chunks, body)
@@ -883,12 +903,11 @@
 
         def add(blocks, own, slots, count, chunk, target):
             total = blocks[0, pl.ds(pl.multiple_of(own * chunk, 16), chunk), :].astype(f32)
-            total = lax.fori_loop(
+            total = add_up(
                 1,
                 count,
-                lambda k, acc: acc
-                + slots[0, pl.ds(pl.multiple_of(k * chunk, 16), chunk), :].astype(f32),
                 total,
+                lambda k: slots[0, pl.ds(aligned(k * chunk), chunk), :].astype(f32),
             )
             self.total[pl.ds(pl.multiple_of(target, 16), chunk), :] = total.astype(bf16)
 
@@ -994,9 +1013,10 @@
         for l in range(layers):
             clear(env, l)
             for i, ref in enumerate(
-                (ln1_gain, ln1_bias, lepe_b, proj_b, ln2_gain, ln2_bias, fc1_b, fc2_b)
+                (ln1_gain, ln1_bias, lepe_b, proj_b, ln2_gain, ln2_bias, fc1_b, fc2_b, ln2_gain)
             ):
-                vec[l, i : i + 1, : ref.shape[1]] = ref[l : l + 1, :]
+                scale = ROOT_HALF if i in (5, 6, 8) else 1.0
+                vec[l, i : i + 1, : ref.shape[1]] = ref[l : l + 1, :] * np.float32(scale)
         stage[...] = jnp.zeros(stage.shape, f32)
 
     def last_image(body):
@@ -1072,7 +1092,7 @@
             pltpu.make_async_copy(packed[which], totals[which], sem_out.at[which]).wait()
 
 
-def last_kernel(factor, crop_side, x, e, total1, total2, total3, out, input_grad, *refs):
+def last_kernel(factor, images, crop_side, x, e, total1, total2, total3, out, input_grad, *refs):
     g_gain1, g_bias1, g_qkv, g_lepe, g_lepe_b, g_proj, g_proj_b = refs[:7]
     g_gain2, g_bias2, g_fc1, g_fc1_b, g_fc2, g_fc2_b = refs[7:13]
     stage, held1, held2, held3, w_qkv, w_proj, w_fc1, w_fc2, sem_in, sem_out = refs[13:]
@@ -1097,9 +1117,10 @@
         at = 0
         for i in which:
             ref = big[i][0]
+            scale = factor * (1.0, 1.0, 1.0 / ROOT_HALF, ROOT_HALF)[i]
             rows, width = ref.shape[1:]
             for lane in range(0, width, GROUP):
-                ref[l, :, lane : lane + GROUP] = packed[at : at + rows, :].astype(f32) * factor
+                ref[l, :, lane : lane + GROUP] = packed[at : at + rows, :].astype(f32) * scale
                 at += rows
             stores[l][i].start()
         return at
@@ -1120,6 +1141,9 @@
         at = 0
         for l in range(1, layers):
             at += unpack(held1.at[at:] if at else held1, l, range(4))
+
+    @pl.when(image == min(1, images - 1))
+    def _():
         loads[1].wait()
         unpack(held2, 0, (2, 3, 1))
         loads[2].wait()
@@ -1202,7 +1226,7 @@
             pltpu.VMEM((ROWS, dim), f32),
             pltpu.VMEM((ROWS, dim), f32),
             pltpu.VMEM((ROWS, dim), f32),
-            pltpu.VMEM((layers, 8, ff), f32),
+            pltpu.VMEM((layers, 16, ff), f32),
         ]
         + [scratch for rows in parts for scratch in grid.scratch(rows)],
         compiler_params=pltpu.CompilerParams(
@@ -1216,7 +1240,7 @@
     factor = 1.0 / math.sqrt(devices * images * tok)
     big = (2, 5, 9, 11)
     return pl.pallas_call(
-        partial(last_kernel, factor),
+        partial(last_kernel, factor, images),
         grid=(images,),
         out_shape=[
             jax.ShapeDtypeStruct(tokens.shape, bf16),

time: 147 us -> 144 us (0.980)
  Pallas kernels: 143 us -> 141 us
    pallas_call x1, Pallas kernels: 134 us -> 132 us  [local(): pl.pallas_call(partial(main_kernel, grid), grid=(images,), out_shape=[jax...]
where the time goes in v5:
time: 144 us
  Pallas kernels  141 us (98%)
  local copies, waits for them, and re-layouts  2.72 us (2%)
    pallas_call x1, Pallas kernels, local(): pl.pallas_call(partial(main_kernel, grid), grid=(images,), out_shape=[jax...  132 us
    pallas_call x1, Pallas kernels, local(): pl.pallas_call(partial(last_kernel, factor, images), grid=(images,), out_...  8.63 us

profile of v5, /device:TPU:0, one launch (start us, length us, event | category | flops | bytes accessed | tf_op | source)
XLA Modules:
  0.0 144.0 jit_solution(17190088359677977811)
XLA Ops:
  0.6 1.3 copy.31.lepe_w
  2.0 132.0 %shard_map.271 = (bf16[4,736,256]{2,1,0:T(8,128)(2,1)}, f32[4,736,256]{2,1,0:T(8,128)}, bf16[6144,128]{1,0:T(8,128)(2,1)}, bf16[4608,128]{1,0:T(8,128)(2,1)}, bf16[2048,128]{1,0:T(8,128)(2,1)}) custom-call(s32[4,8]{1,0:T(4,128)} %crop_side.3, bf16[4,608,256]{2,1,0:T(8,128)(2,1)} %tokens.1, bf16[4,608,256]{2,1,0:T(8,128)(2,1)} %cotangent.1, ...), custom_call_target="tpu_custom_call" | custom-call | tf_op jit(solution)/shard_map/pallas_call | solution.py:1205
  134.0 8.6 %shard_map.272 = (bf16[4,608,256]{2,1,0:T(8,128)(2,1)}, f32[4,608,256]{2,1,0:T(8,128)}, f32[2,256]{1,0:T(2,128)}, f32[2,256]{1,0:T(2,128)}, f32[2,256,768]{2,1,0...) custom-call(s32[4,8]{1,0:T(4,128)} %crop_side.3, ...), custom_call_target="tpu_custom_call" | custom-call | tf_op jit(solution)/shard_map/pallas_call | solution.py:1242
  142.7 1.4 copy.32
